TPU v7x, 32 devices: a whole 2x2x4 slice. The times are simulated.
32 devices in a mesh: pipe: 2 (over core), row: 4 (over y, x), col: 4 (over z).
Axes of the slice: x: 2, y: 2, z: 4, core: 2. Of those that a mesh axis runs over, the one named last changes fastest.
Arguments:
- section_input: float32 [2, 4096, 768], P(None, ('row', 'col')), may hold values from -6 to 6
- cotangent: float32 [2, 4096, 768], P(None, ('row', 'col')), may hold values from -6 to 6
- qkv_weight: bfloat16 [2, 768, 2304], P('pipe', ('row', 'col')), may hold values from -0.21875 to 0.21875
- out_weight: bfloat16 [2, 768, 768], P('pipe', ('row', 'col')), may hold values from -1 to 1
- router_weight: bfloat16 [2, 768, 64], P('pipe', ('row', 'col')), may hold values from -0.15625 to 0.15625
- gain_attn: bfloat16 [2, 768], P('pipe', ('row', 'col')), may hold values from 0.25 to 1.75
- gain_moe: bfloat16 [2, 768], P('pipe', ('row', 'col')), may hold values from 0.25 to 1.75
- rel_bias: bfloat16 [2, 384], P('pipe', ('row', 'col')), may hold values from -6 to 6
- expert_in: bfloat16 [2, 64, 768, 3072], P('pipe', 'row', None, 'col'), may hold values from -0.21875 to 0.21875
- expert_out: bfloat16 [2, 64, 3072, 768], P('pipe', 'row', 'col'), may hold values from -0.21875 to 0.21875
- routes: int32 [2, 2, 4096, 2], P('pipe', None, ('row', 'col')), may hold values from 0 to 63, all different within a row; in each aligned block of 256 rows (0 to 255, 256 to 511, ..., all dimensions but the last counted through in order) at most 12 rows name the same one
- doc_ids: int32 [2, 4096], P(None, 'row'), may hold values from 0 to 3, as said below
- buckets: int32 [1024], replicated, may hold values from 0 to 31, never falling along the last dimension, each value on 1 to 64 neighbouring positions
Outputs:
- section_outputs: float32 [2, 2, 4096, 768], P('pipe', None, ('row', 'col'))
- input_grads: float32 [2, 2, 4096, 768], P('pipe', None, ('row', 'col'))
- grad_qkv_weight: float32 [2, 768, 2304], P('pipe', ('row', 'col'))
- grad_out_weight: float32 [2, 768, 768], P('pipe', ('row', 'col'))
- grad_router_weight: float32 [2, 768, 64], P('pipe', ('row', 'col'))
- grad_gain_attn: float32 [2, 768], P('pipe', ('row', 'col'))
- grad_gain_moe: float32 [2, 768], P('pipe', ('row', 'col'))
- grad_rel_bias: float32 [2, 384], P('pipe', ('row', 'col'))
- grad_expert_in: float32 [2, 64, 768, 3072], P('pipe', 'row', None, 'col')
- grad_expert_out: float32 [2, 64, 3072, 768], P('pipe', 'row', 'col')
Inputs may be any that keep to these rules, and one draw needn't show every extreme that they name: `routes`: each token names 2 different experts; in each aligned block of 256 rows (the tokens of one device, sections and micro-batches in order) no expert is named more than 12 times, a bound that some block reaches. `doc_ids`: numbers the documents of each sequence from 0 at its first position, never falling and rising by at most one from a position to the next; for every index of row one of its 2 sequences is a single document. `buckets`: never falling with the distance; every bucket is used.
All inputs are finite; a program needn't handle non-finite values.
Results may differ from a plain program's by a relative error of at most 0.025.
Values may be sent and summed in bfloat16 or wider, within the bound.
No kernel may reach another device: no remote copies, remote signals or barrier semaphores. Data moves between devices by JAX's collectives and lax.ppermute only.
A program may use at most 576 MiB of HBM per device.

v0:
```python
import jax
import jax.numpy as jnp
from jax import lax
from jax.sharding import PartitionSpec as P

HEADS = 12
HEAD_DIM = 64
EXPERTS = 64
TOP = 2
NBUCKET = 32


EPS = 1e-06
MASKED = -1e30
HIGH = lax.Precision.HIGHEST


def from_partner(value, axis, distance):
    return lax.ppermute(value, axis, [(i, i ^ 1 << distance) for i in range(lax.axis_size(axis))])


def norm_scale(stream, norm_gain):
    return stream * lax.rsqrt(jnp.mean(stream * stream, axis=-1, keepdims=True) + EPS) * norm_gain


def bias_rows(table_flat, buckets, offset, queries):
    length = buckets.shape[0]
    one_hot = (buckets[:, None] == jnp.arange(NBUCKET, dtype=jnp.int32)[None, :]).astype(
        jnp.float32
    )
    by_dist = jnp.dot(
        one_hot,
        table_flat.reshape(NBUCKET, HEADS),
        precision=HIGH,
        preferred_element_type=jnp.float32,
    ).T
    padded = jnp.pad(by_dist, ((0, 0), (length, queries)))
    diagonal = lax.dynamic_slice_in_dim(padded, offset + 1, queries + length - 1, 1)
    tiled = jnp.broadcast_to(diagonal[:, None, :], (HEADS, queries, queries + length - 1)).reshape(
        HEADS, -1
    )
    tiled = jnp.pad(tiled, ((0, 0), (0, queries))).reshape(HEADS, queries, queries + length)
    return jnp.flip(tiled[:, :, :length], axis=2)


def slot_tables(route_rows, capacity):
    flat_routes = route_rows.reshape(-1)
    one_hot = (flat_routes[:, None] == jnp.arange(EXPERTS, dtype=jnp.int32)[None, :]).astype(
        jnp.int32
    )
    running = jnp.cumsum(one_hot, axis=0)
    slot_index = jnp.sum((running - 1) * one_hot, axis=1)
    position = (flat_routes * capacity + slot_index).reshape(-1, TOP)
    columns = jnp.arange(EXPERTS * capacity, dtype=jnp.int32)
    return [(position[:, k : k + 1] == columns[None, :]).astype(jnp.bfloat16) for k in range(TOP)]


def attention_scores(queries, key_rows, pos_bias, allowed):
    raw_scores = jnp.einsum(
        "sqhd,skhd->shqk", queries, key_rows, preferred_element_type=jnp.float32
    )
    return jnp.where(allowed, raw_scores * HEAD_DIM ** (-0.5) + pos_bias[None], MASKED)


def other_section(payload):
    return from_partner(payload.astype(jnp.bfloat16), "pipe", 0).astype(payload.dtype)


def expert_trip(outgoing, worker):
    arrived = lax.all_to_all(outgoing, "row", split_axis=0, concat_axis=0, tiled=True)
    gathered = lax.all_gather(arrived[None], "col", axis=0, tiled=True)
    partial_value, retained = worker(gathered)
    pieces = lax.all_to_all(
        lax.all_to_all(
            partial_value.astype(jnp.bfloat16), "row", split_axis=1, concat_axis=1, tiled=True
        ),
        "col",
        split_axis=0,
        concat_axis=0,
        tiled=True,
    ).astype(partial_value.dtype)
    homeward = jnp.sum(pieces, axis=0).astype(jnp.bfloat16)
    return (homeward, retained)


def expert_forward(weight_in, weight_out):

    def worker(gathered):
        hidden = jnp.einsum(
            "abecd,edf->abecf", gathered, weight_in, preferred_element_type=jnp.float32
        )
        activated = jax.nn.gelu(hidden).astype(jnp.bfloat16)
        partial_value = jnp.einsum(
            "abecf,efd->abecd", activated, weight_out, preferred_element_type=jnp.float32
        )
        return (partial_value, (gathered, hidden))

    return worker


def expert_backward(weight_in, weight_out, gathered, hidden):

    def worker(grad_rows):
        activated, gelu_back = jax.vjp(jax.nn.gelu, hidden)
        grad_act = jnp.einsum(
            "abecd,efd->abecf", grad_rows, weight_out, preferred_element_type=jnp.float32
        )
        grad_weight_out = jnp.einsum(
            "abecf,abecd->efd",
            activated.astype(jnp.bfloat16),
            grad_rows,
            preferred_element_type=jnp.float32,
        )
        grad_hidden = gelu_back(grad_act)[0].astype(jnp.bfloat16)
        grad_weight_in = jnp.einsum(
            "abecd,abecf->edf", gathered, grad_hidden, preferred_element_type=jnp.float32
        )
        partial_value = jnp.einsum(
            "abecf,edf->abecd", grad_hidden, weight_in, preferred_element_type=jnp.float32
        )
        return (partial_value, (grad_weight_in, grad_weight_out))

    return worker


def on_device(
    section_input,
    cotangent,
    qkv_weight,
    out_weight,
    router_weight,
    gain_attn,
    gain_moe,
    rel_bias,
    expert_in,
    expert_out,
    routes,
    doc_ids,
    buckets,
):
    section_index = lax.axis_index("pipe")
    col_index = lax.axis_index("col")
    row_count = lax.axis_size("row")
    col_count = lax.axis_size("col")
    micro_count = section_input.shape[0]
    tokens = section_input.shape[1]
    model_width = section_input.shape[2]
    length = buckets.shape[0]
    piece_len = length // col_count
    sequences = tokens // piece_len
    capacity = 3 * tokens * TOP // (2 * EXPERTS)
    local_experts = expert_in.shape[1]
    qkv_full, out_full, router_full, gain_one, gain_two, table_flat = (
        lax.all_gather(qkv_weight[0], ("row", "col"), axis=0, tiled=True),
        lax.all_gather(out_weight[0], ("row", "col"), axis=0, tiled=True),
        lax.all_gather(router_weight[0], ("row", "col"), axis=0, tiled=True),
        lax.all_gather(gain_attn[0], ("row", "col"), axis=0, tiled=True),
        lax.all_gather(gain_moe[0], ("row", "col"), axis=0, tiled=True),
        lax.all_gather(rel_bias[0], ("row", "col"), axis=0, tiled=True),
    )
    gain_one = gain_one.astype(jnp.float32)
    gain_two = gain_two.astype(jnp.float32)
    weight_in = expert_in[0]
    weight_out = expert_out[0]
    section_routes = routes[0]
    offset = col_index * piece_len
    pos_bias, bias_back = jax.vjp(
        lambda table_value: bias_rows(table_value, buckets, offset, piece_len),
        table_flat.astype(jnp.float32),
    )
    query_place = offset + jnp.arange(piece_len, dtype=jnp.int32)
    causal = query_place[:, None] >= jnp.arange(length, dtype=jnp.int32)[None, :]
    expert_ids = jnp.arange(EXPERTS, dtype=jnp.int32)[None, :]
    outputs = jnp.zeros((micro_count, tokens, model_width), jnp.float32)
    carried = jnp.zeros((tokens, model_width), jnp.float32)
    kept_list = []
    for moment in range(micro_count + 1):
        micro_index = moment - section_index
        is_valid = (micro_index >= 0) & (micro_index < micro_count)
        micro_index = jnp.clip(micro_index, 0, micro_count - 1)
        own_input = lax.dynamic_index_in_dim(section_input, micro_index, 0, keepdims=False)
        stream = jnp.where(section_index == 0, own_input, carried)
        route_rows = lax.dynamic_index_in_dim(section_routes, micro_index, 0, keepdims=False)
        doc_block = lax.dynamic_index_in_dim(doc_ids, micro_index, 0, keepdims=False).reshape(
            col_count, sequences, piece_len
        )
        doc_keys = jnp.swapaxes(doc_block, 0, 1).reshape(sequences, length)
        doc_query = lax.dynamic_index_in_dim(doc_block, col_index, 0, keepdims=False)
        allowed = causal[None, None] & (doc_query[:, None, :, None] == doc_keys[:, None, None, :])
        normed_attn = norm_scale(stream, gain_one).astype(jnp.bfloat16)
        qkv_rows = jnp.dot(normed_attn, qkv_full, preferred_element_type=jnp.float32).astype(
            jnp.bfloat16
        )
        queries = qkv_rows[:, :model_width].reshape(sequences, piece_len, HEADS, HEAD_DIM)
        key_rows = lax.all_gather(
            qkv_rows[:, model_width : 2 * model_width].reshape(sequences, piece_len, model_width),
            "col",
            axis=1,
            tiled=True,
        )
        value_rows = lax.all_gather(
            qkv_rows[:, 2 * model_width :].reshape(sequences, piece_len, model_width),
            "col",
            axis=1,
            tiled=True,
        )
        key_rows = key_rows.reshape(sequences, length, HEADS, HEAD_DIM)
        value_rows = value_rows.reshape(sequences, length, HEADS, HEAD_DIM)
        scores = attention_scores(queries, key_rows, pos_bias, allowed)
        maxima = jnp.max(scores, axis=-1, keepdims=True)
        weights = jnp.exp(scores - maxima)
        totals = jnp.sum(weights, axis=-1, keepdims=True)
        log_total = maxima + jnp.log(totals)
        probability = (weights / totals).astype(jnp.bfloat16)
        attended = jnp.einsum(
            "shqk,skhd->sqhd", probability, value_rows, preferred_element_type=jnp.float32
        )
        attended = attended.reshape(tokens, model_width).astype(jnp.bfloat16)
        after_attn = stream + jnp.dot(attended, out_full, preferred_element_type=jnp.float32)
        normed_moe = norm_scale(after_attn, gain_two).astype(jnp.bfloat16)
        logits = jnp.dot(normed_moe, router_full, preferred_element_type=jnp.float32)
        chosen = jnp.stack(
            [
                jnp.sum(jnp.where(route_rows[:, k : k + 1] == expert_ids, logits, 0.0), axis=1)
                for k in range(TOP)
            ],
            axis=1,
        )
        chosen = jnp.exp(chosen - jnp.max(chosen, axis=1, keepdims=True))
        gate_weights = chosen / jnp.sum(chosen, axis=1, keepdims=True)
        tables = slot_tables(route_rows, capacity)
        outgoing = jnp.zeros((EXPERTS * capacity, model_width), jnp.float32)
        for table_k in tables:
            outgoing = outgoing + jnp.einsum(
                "tc,td->cd", table_k, normed_moe, preferred_element_type=jnp.float32
            )
        outgoing = outgoing.astype(jnp.bfloat16).reshape(
            row_count, local_experts, capacity, model_width
        )
        homeward, retained = expert_trip(outgoing, expert_forward(weight_in, weight_out))
        returned = homeward.reshape(EXPERTS * capacity, model_width)
        result = after_attn
        for k in range(TOP):
            result = result + gate_weights[:, k : k + 1] * jnp.dot(
                tables[k], returned, preferred_element_type=jnp.float32
            )
        kept_state = (
            stream,
            after_attn,
            normed_attn,
            qkv_rows,
            key_rows,
            value_rows,
            log_total,
            allowed,
            attended,
            normed_moe,
            gate_weights,
            route_rows,
            returned,
        ) + retained
        result, kept_state = (result, kept_state)
        outputs = jnp.where(
            is_valid, lax.dynamic_update_index_in_dim(outputs, result, micro_index, 0), outputs
        )
        kept_list.append(kept_state)
        if moment < micro_count:
            carried = other_section(result)
    input_grads = jnp.zeros_like(outputs)
    carried = jnp.zeros((tokens, model_width), jnp.float32)
    dense_sums = None
    expert_totals = None
    for moment in range(micro_count + 1):
        micro_index = moment - 1 + section_index
        is_valid = (micro_index >= 0) & (micro_index < micro_count)
        micro_index = jnp.clip(micro_index, 0, micro_count - 1)
        own_grad = lax.dynamic_index_in_dim(cotangent, micro_index, 0, keepdims=False)
        former = kept_list[max(moment - 1, 0)]
        latter = kept_list[min(moment + 1, micro_count)]
        kept_state = jax.tree.map(
            lambda earlier, later_state: jnp.where(section_index == 0, earlier, later_state),
            former,
            latter,
        )
        grad_result = jnp.where(section_index == 1, own_grad, carried)
        (
            backward_stream,
            backward_after_attn,
            backward_normed_attn,
            backward_qkv_rows,
            backward_key_rows,
            backward_value_rows,
            backward_log_total,
            backward_allowed,
            backward_attended,
            backward_normed_moe,
            backward_gate_weights,
            backward_route_rows,
            backward_returned,
            gathered,
            hidden,
        ) = kept_state
        backward_tables = slot_tables(backward_route_rows, capacity)
        grad_slots = jnp.zeros((EXPERTS * capacity, model_width), jnp.float32)
        gate_parts = []
        for backward_k in range(TOP):
            picked = jnp.dot(
                backward_tables[backward_k], backward_returned, preferred_element_type=jnp.float32
            )
            gate_parts.append(jnp.sum(grad_result * picked, axis=1))
            grad_slots = grad_slots + jnp.einsum(
                "tc,td->cd",
                backward_tables[backward_k].astype(jnp.float32),
                backward_gate_weights[:, backward_k : backward_k + 1] * grad_result,
                precision=HIGH,
                preferred_element_type=jnp.float32,
            )
        grad_gate = jnp.stack(gate_parts, axis=1)
        grad_chosen = backward_gate_weights * (
            grad_gate - jnp.sum(backward_gate_weights * grad_gate, axis=1, keepdims=True)
        )
        grad_logits = jnp.zeros((tokens, EXPERTS), jnp.float32)
        for backward_k in range(TOP):
            grad_logits = grad_logits + jnp.where(
                backward_route_rows[:, backward_k : backward_k + 1] == expert_ids,
                grad_chosen[:, backward_k : backward_k + 1],
                0.0,
            )
        grad_logits = grad_logits.astype(jnp.bfloat16)
        backward_outgoing = grad_slots.astype(jnp.bfloat16).reshape(
            row_count, local_experts, capacity, model_width
        )
        backward_homeward, expert_terms = expert_trip(
            backward_outgoing, expert_backward(weight_in, weight_out, gathered, hidden)
        )
        grad_rows = backward_homeward.reshape(EXPERTS * capacity, model_width)
        grad_normed = jnp.einsum(
            "te,de->td", grad_logits, router_full, preferred_element_type=jnp.float32
        )
        for backward_k in range(TOP):
            grad_normed = grad_normed + jnp.dot(
                backward_tables[backward_k], grad_rows, preferred_element_type=jnp.float32
            )
        grad_router = jnp.einsum(
            "td,te->de", backward_normed_moe, grad_logits, preferred_element_type=jnp.float32
        )
        unused, norm_back = jax.vjp(norm_scale, backward_after_attn, gain_two)
        grad_after, grad_gain_two = norm_back(grad_normed)
        grad_after = grad_result + grad_after
        grad_branch = grad_after.astype(jnp.bfloat16)
        grad_out_proj = jnp.einsum(
            "tc,td->cd", backward_attended, grad_branch, preferred_element_type=jnp.float32
        )
        grad_attended = jnp.einsum(
            "td,cd->tc", grad_branch, out_full, preferred_element_type=jnp.float32
        )
        grad_attended = grad_attended.astype(jnp.bfloat16).reshape(
            sequences, piece_len, HEADS, HEAD_DIM
        )
        backward_queries = backward_qkv_rows[:, :model_width].reshape(
            sequences, piece_len, HEADS, HEAD_DIM
        )
        backward_scores = attention_scores(
            backward_queries, backward_key_rows, pos_bias, backward_allowed
        )
        backward_probability = jnp.exp(backward_scores - backward_log_total)
        grad_values = jnp.einsum(
            "shqk,sqhd->skhd",
            backward_probability.astype(jnp.bfloat16),
            grad_attended,
            preferred_element_type=jnp.float32,
        )
        grad_prob = jnp.einsum(
            "sqhd,skhd->shqk",
            grad_attended,
            backward_value_rows,
            preferred_element_type=jnp.float32,
        )
        grad_scores = backward_probability * (
            grad_prob - jnp.sum(backward_probability * grad_prob, axis=-1, keepdims=True)
        )
        grad_table = bias_back(jnp.sum(grad_scores, axis=0))[0]
        grad_raw = (grad_scores * HEAD_DIM ** (-0.5)).astype(jnp.bfloat16)
        grad_queries = jnp.einsum(
            "shqk,skhd->sqhd", grad_raw, backward_key_rows, preferred_element_type=jnp.float32
        )
        grad_keys = jnp.einsum(
            "shqk,sqhd->skhd", grad_raw, backward_queries, preferred_element_type=jnp.float32
        )
        grad_key_sum = lax.psum_scatter(
            grad_keys.reshape(sequences, length, model_width).astype(jnp.bfloat16),
            "col",
            scatter_dimension=1,
            tiled=True,
        ).astype(jnp.float32)
        grad_value_sum = lax.psum_scatter(
            grad_values.reshape(sequences, length, model_width).astype(jnp.bfloat16),
            "col",
            scatter_dimension=1,
            tiled=True,
        ).astype(jnp.float32)
        grad_qkv = jnp.concatenate(
            [
                grad_queries.reshape(tokens, model_width).astype(jnp.bfloat16),
                grad_key_sum.reshape(tokens, model_width).astype(jnp.bfloat16),
                grad_value_sum.reshape(tokens, model_width).astype(jnp.bfloat16),
            ],
            axis=1,
        )
        grad_qkv_proj = jnp.einsum(
            "tc,td->cd", backward_normed_attn, grad_qkv, preferred_element_type=jnp.float32
        )
        grad_normed_attn = jnp.einsum(
            "td,cd->tc", grad_qkv, qkv_full, preferred_element_type=jnp.float32
        )
        unused, norm_back_one = jax.vjp(norm_scale, backward_stream, gain_one)
        grad_stream, grad_gain_one = norm_back_one(grad_normed_attn)
        dense_terms = (
            grad_qkv_proj,
            grad_out_proj,
            grad_router,
            grad_gain_one,
            grad_gain_two,
            grad_table,
        )
        grad_stream, dense_terms, expert_terms = (
            grad_after + grad_stream,
            dense_terms,
            expert_terms,
        )
        scale_flag = is_valid.astype(jnp.float32)
        dense_terms = jax.tree.map(lambda term_value: term_value * scale_flag, dense_terms)
        expert_terms = jax.tree.map(lambda term_value: term_value * scale_flag, expert_terms)
        if moment == 0:
            dense_sums = dense_terms
            expert_totals = expert_terms
        else:
            dense_sums = jax.tree.map(jnp.add, dense_sums, dense_terms)
            expert_totals = jax.tree.map(jnp.add, expert_totals, expert_terms)
        input_grads = jnp.where(
            is_valid,
            lax.dynamic_update_index_in_dim(input_grads, grad_stream, micro_index, 0),
            input_grads,
        )
        if moment < micro_count:
            carried = other_section(grad_stream)
    dense_total = (
        lax.psum_scatter(dense_sums[0], ("row", "col"), scatter_dimension=0, tiled=True),
        lax.psum_scatter(dense_sums[1], ("row", "col"), scatter_dimension=0, tiled=True),
        lax.psum_scatter(dense_sums[2], ("row", "col"), scatter_dimension=0, tiled=True),
        lax.psum_scatter(dense_sums[3], ("row", "col"), scatter_dimension=0, tiled=True),
        lax.psum_scatter(dense_sums[4], ("row", "col"), scatter_dimension=0, tiled=True),
        lax.psum_scatter(dense_sums[5], ("row", "col"), scatter_dimension=0, tiled=True),
    )
    return (
        outputs[None],
        input_grads[None],
        dense_total[0][None],
        dense_total[1][None],
        dense_total[2][None],
        dense_total[3][None],
        dense_total[4][None],
        dense_total[5][None],
        expert_totals[0][None],
        expert_totals[1][None],
    )


def solution(mesh):
    return jax.shard_map(
        on_device,
        mesh=mesh,
        in_specs=(
            P(None, ("row", "col"), None),
            P(None, ("row", "col"), None),
            P("pipe", ("row", "col"), None),
            P("pipe", ("row", "col"), None),
            P("pipe", ("row", "col"), None),
            P("pipe", ("row", "col")),
            P("pipe", ("row", "col")),
            P("pipe", ("row", "col")),
            P("pipe", "row", None, "col"),
            P("pipe", "row", "col", None),
            P("pipe", None, ("row", "col"), None),
            P(None, "row"),
            P(),
        ),
        out_specs=(
            P("pipe", None, ("row", "col"), None),
            P("pipe", None, ("row", "col"), None),
            P("pipe", ("row", "col"), None),
            P("pipe", ("row", "col"), None),
            P("pipe", ("row", "col"), None),
            P("pipe", ("row", "col")),
            P("pipe", ("row", "col")),
            P("pipe", ("row", "col")),
            P("pipe", "row", None, "col"),
            P("pipe", "row", "col", None),
        ),
        check_vma=False,
    )
```

profile of v0, /device:TPU:0, one launch (start us, length us, event | category | flops | bytes accessed | tf_op | source)
XLA Modules:
  0.0 3401.0 jit_solution(17834978567887970142)
XLA Ops:
  13.1 45.1 %all-reduce.12 = (bf16[768]{0:T(1024)(128)(2,1)S(1)}, bf16[384]{0:T(512)(128)(2,1)S(1)}, bf16[768]{0:T(1024)(128)(2,1)S(1)}) all-reduce(bf16[768]{0:T(1024)(128)(2,1)S(1)} %dynamic-update-slice.8, bf16[384]{0:T(512)(128)(2,1)S(1)} %dynamic-update-slice.9, ...), channel_id=2, replica_groups=mesh['pipe'=2,'row'=4,'col'=4] {'row','col'}, use_global_device_ids=true, to_apply=%add.5 | all-reduce | flops 1920 | bytes 7680
  61.1 23.9 all-gather.33.cloned.1.call-done
  100.6 26.1 reshape.1434
  156.5 101.0 %rev.14 = f32[12,256,1024]{2,1,0:T(8,128)} reverse(f32[12,256,1024]{2,1,0:T(8,128)} %slice.277), dimensions={2} | reverse | bytes 25165824 | tf_op jit(solution)/shard_map/jvp(jit(_flip))/rev | solution.py:43
  307.4 17.9 all_to_all.90
  325.3 88.7 %all-gather.41.cloned.1.call-done = bf16[16,16,12,768]{3,1,2,0:T(8,128)(2,1)} async-done(((bf16[4,16,12,768]{3,1,2,0:T(8,128)(2,1)}), bf16[16,16,12,768]{3,1,2,0:T(8,128)(2,1)}) %all-gather.41.cloned.1.call-update) | async-done | bytes 4718608 | tf_op jit(solution)/shard_map/all_gather | solution.py:71
  435.9 16.5 convert_bitcast_fusion.5
  457.8 57.0 %all_to_all.91 = bf16[4,4,16,12,768]{4,2,3,0,1:T(8,128)(2,1)S(1)} all-to-all(bf16[4,4,16,12,768]{4,2,3,0,1:T(8,128)(2,1)S(1)} %copy.266), channel_id=1, replica_groups=mesh['pipe'=2,'row'=4,'col'=4] {'row'}, dimensions={1} | all-to-all | bytes 9437184 | tf_op jit(solution)/shard_map/all_to_all | solution.py:74
  522.4 133.6 %all-gather.7 = bf16[1,768,64]{2,1,0:T(8,128)(2,1)S(1)} all-gather(bf16[1,48,64]{2,1,0:T(8,128)(2,1)S(1)} %copy-done.174), channel_id=9, replica_groups=mesh['pipe'=2,'row'=4,'col'=4] {'row','col'}, dimensions={1}, use_global_device_ids=true | all-gather | bytes 104448 | tf_op jit(solution)/shard_map/all_gather | solution.py:156
  678.2 33.2 all-gather.45.cloned.1.call-done
  727.2 22.3 all-gather.43.cloned.1.call-done
  761.6 19.1 all_to_all.92
  780.8 87.3 %all-gather.47.cloned.1.call-done = bf16[16,16,12,768]{3,1,2,0:T(8,128)(2,1)} async-done(((bf16[4,16,12,768]{3,1,2,0:T(8,128)(2,1)}), bf16[16,16,12,768]{3,1,2,0:T(8,128)(2,1)}) %all-gather.47.cloned.1.call-update) | async-done | bytes 4718608 | tf_op jit(solution)/shard_map/all_gather | solution.py:71
  889.9 16.3 convert_bitcast_fusion.4
  911.6 57.0 %all_to_all.93 = bf16[4,4,16,12,768]{4,2,3,0,1:T(8,128)(2,1)S(1)} all-to-all(bf16[4,4,16,12,768]{4,2,3,0,1:T(8,128)(2,1)S(1)} %copy.281), channel_id=1, replica_groups=mesh['pipe'=2,'row'=4,'col'=4] {'row'}, dimensions={1} | all-to-all | bytes 9437184 | tf_op jit(solution)/shard_map/all_to_all | solution.py:74
  976.8 102.7 %all-to-all-done.5 = bf16[4,4,16,12,768]{4,2,3,1,0:T(8,128)(2,1)} async-done(((bf16[4,4,16,12,768]{4,2,3,1,0:T(8,128)(2,1)}), bf16[4,4,16,12,768]{4,2,3,1,0:T(8,128)(2,1)}, u32[]{:S(2)}, u32[]{:S(2)}) %all-to-all-start.5) | async-done | bytes 4718624 | tf_op jit(solution)/shard_map/all_to_all | solution.py:73
  1108.5 19.3 all_to_all.94
  1140.6 35.7 %all-gather.51.cloned.1.call-done = bf16[1024,768]{1,0:T(8,128)(2,1)} async-done(((bf16[256,768]{1,0:T(8,128)(2,1)}), bf16[1024,768]{1,0:T(8,128)(2,1)}) %all-gather.51.cloned.1.call-update) | async-done | bytes 1572880 | tf_op jit(solution)/shard_map/all_gather | solution.py:195
  1195.6 19.1 all_to_all.95
  1214.8 51.4 %all-gather.55.cloned.1.call-done = bf16[16,16,12,768]{3,1,2,0:T(8,128)(2,1)} async-done(((bf16[4,16,12,768]{3,1,2,0:T(8,128)(2,1)}), bf16[16,16,12,768]{3,1,2,0:T(8,128)(2,1)}) %all-gather.55.cloned.1.call-update) | async-done | bytes 4718608 | tf_op jit(solution)/shard_map/all_gather | solution.py:71
  1287.3 33.0 multiply_convert_fusion.5
  1338.3 57.2 %all_to_all.96 = bf16[4,4,16,12,768]{4,2,3,0,1:T(8,128)(2,1)S(1)} all-to-all(bf16[4,4,16,12,768]{4,2,3,0,1:T(8,128)(2,1)S(1)} %copy.306), channel_id=1, replica_groups=mesh['pipe'=2,'row'=4,'col'=4] {'row'}, dimensions={1} | all-to-all | bytes 9437184 | tf_op jit(solution)/shard_map/all_to_all | solution.py:74
  1452.3 54.5 %all-to-all-done.11 = bf16[4,4,16,12,768]{4,2,3,1,0:T(8,128)(2,1)} async-done(((bf16[4,4,16,12,768]{4,2,3,1,0:T(8,128)(2,1)}), bf16[4,4,16,12,768]{4,2,3,1,0:T(8,128)(2,1)}, u32[]{:S(2)}, u32[]{:S(2)}) %all-to-all-start.11) | async-done | bytes 4718624 | tf_op jit(solution)/shard_map/all_to_all | solution.py:73
  1597.6 22.1 reduce-scatter.12.cloned.1.call-done
  1619.7 78.1 %reduce-scatter.10.cloned.1.call-done = bf16[1,256,768]{1,2,0:T(8,128)(2,1)} async-done(((bf16[1,1024,768]{1,2,0:T(8,128)(2,1)}), bf16[1,256,768]{1,2,0:T(8,128)(2,1)}) %reduce-scatter.10.cloned.1.call-update) | async-done | bytes 393232 | tf_op jit(solution)/shard_map/reduce_scatter | solution.py:390
  1739.0 19.3 all_to_all.97
  1758.3 87.1 %all-gather.57.cloned.1.call-done = bf16[16,16,12,768]{3,1,2,0:T(8,128)(2,1)} async-done(((bf16[4,16,12,768]{3,1,2,0:T(8,128)(2,1)}), bf16[16,16,12,768]{3,1,2,0:T(8,128)(2,1)}) %all-gather.57.cloned.1.call-update) | async-done | bytes 4718608 | tf_op jit(solution)/shard_map/all_gather | solution.py:71
  1865.6 32.9 multiply_convert_fusion.4
  1916.5 57.0 %all_to_all.98 = bf16[4,4,16,12,768]{4,2,3,0,1:T(8,128)(2,1)S(1)} all-to-all(bf16[4,4,16,12,768]{4,2,3,0,1:T(8,128)(2,1)S(1)} %copy.318), channel_id=1, replica_groups=mesh['pipe'=2,'row'=4,'col'=4] {'row'}, dimensions={1} | all-to-all | bytes 9437184 | tf_op jit(solution)/shard_map/all_to_all | solution.py:74
  1982.6 101.7 %all-to-all-done.14 = bf16[4,4,16,12,768]{4,2,3,1,0:T(8,128)(2,1)} async-done(((bf16[4,4,16,12,768]{4,2,3,1,0:T(8,128)(2,1)}), bf16[4,4,16,12,768]{4,2,3,1,0:T(8,128)(2,1)}, u32[]{:S(2)}, u32[]{:S(2)}) %all-to-all-start.14) | async-done | bytes 4718624 | tf_op jit(solution)/shard_map/all_to_all | solution.py:73
  2164.5 37.0 %reduce-scatter.14.cloned.1.call-done = bf16[1,256,768]{1,2,0:T(8,128)(2,1)} async-done(((bf16[1,1024,768]{1,2,0:T(8,128)(2,1)}), bf16[1,256,768]{1,2,0:T(8,128)(2,1)}) %reduce-scatter.14.cloned.1.call-update) | async-done | bytes 393232 | tf_op jit(solution)/shard_map/reduce_scatter | solution.py:390
  2217.9 19.5 all_to_all.99
  2247.0 77.5 %all-gather.59.cloned.1.call-done = bf16[16,16,12,768]{3,1,2,0:T(8,128)(2,1)} async-done(((bf16[4,16,12,768]{3,1,2,0:T(8,128)(2,1)}), bf16[16,16,12,768]{3,1,2,0:T(8,128)(2,1)}) %all-gather.59.cloned.1.call-update) | async-done | bytes 4718608 | tf_op jit(solution)/shard_map/all_gather | solution.py:71
  2344.8 33.2 multiply_convert_fusion.3
  2403.3 20.5 fusion.100
  2434.9 21.8 all-to-all-done.16
  2466.6 21.7 fusion.92
  2488.3 101.0 %rev.15 = f32[12,256,1024]{2,1,0:T(8,128)} reverse(f32[12,256,1024]{2,1,0:T(8,128)} %copy-done.3), dimensions={2} | reverse | bytes 25165824 | tf_op jit(solution)/shard_map/transpose(jvp(jit(_flip)))/rev | solution.py:43
  2638.8 31.4 reshape.1473
  2747.2 21.6 fusion.89
  2778.3 20.6 fusion.97
  2798.9 101.0 %rev.16 = f32[12,256,1024]{2,1,0:T(8,128)} reverse(f32[12,256,1024]{2,1,0:T(8,128)} %copy-done.4), dimensions={2} | reverse | bytes 25165824 | tf_op jit(solution)/shard_map/transpose(jvp(jit(_flip)))/rev | solution.py:43
  2949.2 31.3 reshape.1475
  3014.7 48.2 %fusion.4 = f32[1,16,768,768]{3,2,1,0:T(8,128)} fusion(f32[16,768,768,1,1]{2,1,4,3,0:T(8,128)} %fusion.89, f32[16,768,768,1,1]{2,1,4,3,0:T(8,128)} %fusion.92, f32[]{:T(128)S(6)} %convert_element_type.621, f32[]{:T(128)S(6)} %convert_element_type.620, f32[]{:T(128)S(6)} %convert_element_type.619, bf16[4,4,16,12,768]{4,2,3,1,0:T(8,128)(2,1)} %get-tuple-element.73, ...), kind=kOutput, calls=%fused_computation.8 | convolution fusion | flops 3671064576 | bytes 122683408 | tf_op jit(solution)/shard_map/abecd,abecf->edf/dot_general | solution.py:115
  3062.9 48.5 %fusion.1 = f32[1,16,768,768]{3,2,1,0:T(8,128)} fusion(f32[16,768,768,1,1]{2,1,4,3,0:T(8,128)} %fusion.97, f32[16,768,768,1,1]{2,1,4,3,0:T(8,128)} %fusion.100, f32[]{:T(128)S(6)} %convert_element_type.621, f32[]{:T(128)S(6)} %convert_element_type.620, f32[]{:T(128)S(6)} %convert_element_type.619, bf16[4,4,16,12,768]{4,2,3,1,0:T(8,128)(2,1)} %bitcast.706, ...), kind=kOutput, calls=%fused_computation.2 | convolution fusion | flops 3671064576 | bytes 122683408 | tf_op jit(solution)/shard_map/abecf,abecd->efd/dot_general | solution.py:108
  3111.3 101.2 %rev.17 = f32[12,256,1024]{2,1,0:T(8,128)} reverse(f32[12,256,1024]{2,1,0:T(8,128)} %copy-done.5), dimensions={2} | reverse | bytes 25165824 | tf_op jit(solution)/shard_map/transpose(jvp(jit(_flip)))/rev | solution.py:43
  3261.8 31.1 reshape.1477
  3312.8 76.2 %all-reduce.11 = (f32[768]{0:T(1024)S(1)}, f32[768]{0:T(1024)S(1)}, f32[384]{0:T(512)S(1)}) all-reduce(f32[768]{0:T(1024)S(1)} %multiply_add_fusion.3, f32[768]{0:T(1024)S(1)} %copy-done.173, f32[384]{0:T(512)S(1)} %copy-done.224), channel_id=29, replica_groups=mesh['pipe'=2,'row'=4,'col'=4] {'row','col'}, use_global_device_ids=true, to_apply=%region_81.82.clone | all-reduce | flops 1920 | bytes 15360
  (939 shorter events, 1020.9 us)
Async XLA Ops:
  7.2 77.9 %all-gather.33.cloned.1.call-start = ((), (), s32[]{:S(2)}) async-start(), calls=%async_computation.36 | async-start | bytes 3760128 | tf_op jit(solution)/shard_map/all_gather | solution.py:154
  7.9 265.5 %all-gather.37.cloned.1.call-start = ((), (), s32[]{:S(2)}) async-start(), calls=%async_computation.38 | async-start | bytes 1966080 | tf_op jit(solution)/shard_map/all_gather | solution.py:195
  58.2 1040.3 %copy-start.129 = (f32[768]{0:T(1024)}, f32[768]{0:T(1024)S(1)}, u32[]{:S(2)}) copy-start(f32[768]{0:T(1024)S(1)} %convert_element_type.627) | copy-start | bytes 9220
  90.2 194.6 %all-gather.35.cloned.1.call-start = ((), (), s32[]{:S(2)}) async-start(), calls=%async_computation.37 | async-start | bytes 1966080 | tf_op jit(solution)/shard_map/all_gather | solution.py:201
  90.9 208.6 %all-gather.39.cloned.1.call-start = ((), (), s32[]{:S(2)}) async-start(), calls=%async_computation.39 | async-start | bytes 1253376 | tf_op jit(solution)/shard_map/all_gather | solution.py:155
  91.5 322.6 %all-gather.41.cloned.1.call-start = ((), (), s32[]{:S(2)}) async-start(), calls=%async_computation.40 | async-start | bytes 5898240 | tf_op jit(solution)/shard_map/all_gather | solution.py:71
  91.6 178.4 %copy-start.151 = (s32[1,1,256,2]{2,3,1,0:T(2,128)}, s32[1,1,256,2]{2,3,1,0:T(2,128)S(1)}, u32[]{:S(2)}) copy-start(s32[1,1,256,2]{2,3,1,0:T(2,128)S(1)} %get-tuple-element.112) | copy-start | bytes 6148
  91.6 178.4 %copy-start.153 = (s32[1,1,256,2]{2,3,1,0:T(2,128)}, s32[1,1,256,2]{2,3,1,0:T(2,128)S(1)}, u32[]{:S(2)}) copy-start(s32[1,1,256,2]{2,3,1,0:T(2,128)S(1)} %get-tuple-element.114) | copy-start | bytes 6148
  258.8 1841.1 %copy-start.125 = (f32[768]{0:T(1024)}, f32[768]{0:T(1024)S(1)}, u32[]{:S(2)}) copy-start(f32[768]{0:T(1024)S(1)} %convert_element_type.628) | copy-start | bytes 9220
  301.7 354.4 %copy-start.33 = (bf16[256,768]{1,0:T(8,128)(2,1)}, bf16[256,768]{1,0:T(8,128)(2,1)S(1)}, u32[]{:S(2)}) copy-start(bf16[256,768]{1,0:T(8,128)(2,1)S(1)} %multiply_convert_fusion.28) | copy-start | bytes 1179652
  517.3 140.3 %all-to-all-start.2 = ((bf16[4,4,16,12,768]{4,2,3,1,0:T(8,128)(2,1)}), bf16[4,4,16,12,768]{4,2,3,1,0:T(8,128)(2,1)}, u32[]{:S(2)}, u32[]{:S(2)}) async-start(bf16[4,4,16,12,768]{4,2,3,1,0:T(8,128)(2,1)} %copy.267), calls=%async_computation.2 | async-start | bytes 9437184 | tf_op jit(solution)/shard_map/all_to_all | solution.py:73
  522.4 189.0 %all-gather.45.cloned.1.call-start = ((), (), s32[]{:S(2)}) async-start(), calls=%async_computation.42 | async-start | bytes 1966080 | tf_op jit(solution)/shard_map/all_gather | solution.py:195
  656.4 434.4 %copy-start.147 = (f32[256]{0:T(256)}, f32[256]{0:T(256)S(1)}, u32[]{:S(2)}) copy-start(f32[256]{0:T(256)S(1)} %get-tuple-element.26) | copy-start | bytes 3076
  656.4 434.4 %copy-start.149 = (f32[256]{0:T(256)}, f32[256]{0:T(256)S(1)}, u32[]{:S(2)}) copy-start(f32[256]{0:T(256)S(1)} %get-tuple-element.27) | copy-start | bytes 3076
  669.6 1.7 collective-permute-start
  677.2 72.3 %all-gather.43.cloned.1.call-start = ((), (), s32[]{:S(2)}) async-start(), calls=%async_computation.41 | async-start | bytes 1966080 | tf_op jit(solution)/shard_map/all_gather | solution.py:201
  677.9 190.1 %all-gather.47.cloned.1.call-start = ((), (), s32[]{:S(2)}) async-start(), calls=%async_computation.43 | async-start | bytes 5898240 | tf_op jit(solution)/shard_map/all_gather | solution.py:71
  759.5 216.9 %copy-start.35 = (bf16[256,768]{1,0:T(8,128)(2,1)}, bf16[256,768]{1,0:T(8,128)(2,1)S(1)}, u32[]{:S(2)}) copy-start(bf16[256,768]{1,0:T(8,128)(2,1)S(1)} %multiply_convert_fusion.26) | copy-start | bytes 1179652
  971.2 108.3 %all-to-all-start.5 = ((bf16[4,4,16,12,768]{4,2,3,1,0:T(8,128)(2,1)}), bf16[4,4,16,12,768]{4,2,3,1,0:T(8,128)(2,1)}, u32[]{:S(2)}, u32[]{:S(2)}) async-start(bf16[4,4,16,12,768]{4,2,3,1,0:T(8,128)(2,1)} %copy.282), calls=%async_computation.5 | async-start | bytes 9437184 | tf_op jit(solution)/shard_map/all_to_all | solution.py:73
  976.3 162.6 %all-gather.49.cloned.1.call-start = ((), (), s32[]{:S(2)}) async-start(), calls=%async_computation.44 | async-start | bytes 1966080 | tf_op jit(solution)/shard_map/all_gather | solution.py:201
  976.4 128.4 %copy-start.175 = (s32[256,1]{0,1:T(1,128)}, s32[256,1]{0,1:T(1,128)S(1)}, u32[]{:S(2)}) copy-start(s32[256,1]{0,1:T(1,128)S(1)} %get-tuple-element.160) | copy-start | bytes 3076
  976.4 129.9 %copy-start.192 = (s32[256,1]{0,1:T(1,128)}, s32[256,1]{0,1:T(1,128)S(1)}, u32[]{:S(2)}) copy-start(s32[256,1]{0,1:T(1,128)S(1)} %get-tuple-element.161) | copy-start | bytes 3076
  1095.0 1.7 collective-permute-start.1
  1103.7 72.6 %all-gather.51.cloned.1.call-start = ((), (), s32[]{:S(2)}) async-start(), calls=%async_computation.45 | async-start | bytes 1966080 | tf_op jit(solution)/shard_map/all_gather | solution.py:195
  1104.2 161.9 %all-gather.55.cloned.1.call-start = ((), (), s32[]{:S(2)}) async-start(), calls=%async_computation.47 | async-start | bytes 5898240 | tf_op jit(solution)/shard_map/all_gather | solution.py:71
  1127.8 278.8 %all-gather.53.cloned.1.call-start = ((), (), s32[]{:S(2)}) async-start(), calls=%async_computation.46 | async-start | bytes 5898240 | tf_op jit(solution)/shard_map/all_gather | solution.py:71
  1193.5 511.1 %copy-start.37 = (bf16[256,768]{1,0:T(8,128)(2,1)}, bf16[256,768]{1,0:T(8,128)(2,1)S(1)}, u32[]{:S(2)}) copy-start(bf16[256,768]{1,0:T(8,128)(2,1)S(1)} %get-tuple-element.97) | copy-start | bytes 1179652
  1398.2 108.7 %all-to-all-start.11 = ((bf16[4,4,16,12,768]{4,2,3,1,0:T(8,128)(2,1)}), bf16[4,4,16,12,768]{4,2,3,1,0:T(8,128)(2,1)}, u32[]{:S(2)}, u32[]{:S(2)}) async-start(bf16[4,4,16,12,768]{4,2,3,1,0:T(8,128)(2,1)} %copy.307), calls=%async_computation.11 | async-start | bytes 9437184 | tf_op jit(solution)/shard_map/all_to_all | solution.py:73
  1506.8 57.5 %all-to-all-start.7 = ((bf16[4,4,16,12,768]{4,2,3,0,1:T(8,128)(2,1)}), bf16[4,4,16,12,768]{4,2,3,0,1:T(8,128)(2,1)}, u32[]{:S(2)}, u32[]{:S(2)}) async-start(bf16[4,4,16,12,768]{4,2,3,0,1:T(8,128)(2,1)} %copy.296), calls=%async_computation.7 | async-start | bytes 9437184 | tf_op jit(solution)/shard_map/all_to_all | solution.py:74
  1511.8 107.8 %reduce-scatter.12.cloned.1.call-start = ((), (), s32[]{:S(2)}) async-start(), calls=%async_computation.28 | async-start | bytes 1966080 | tf_op jit(solution)/shard_map/reduce_scatter | solution.py:396
  1569.3 146.4 %all-to-all-start.8 = ((bf16[4,4,16,12,768]{4,2,3,1,0:T(8,128)(2,1)}), bf16[4,4,16,12,768]{4,2,3,1,0:T(8,128)(2,1)}, u32[]{:S(2)}, u32[]{:S(2)}) async-start(bf16[4,4,16,12,768]{4,2,3,1,0:T(8,128)(2,1)} %copy.297), calls=%async_computation.8 | async-start | bytes 9437184 | tf_op jit(solution)/shard_map/all_to_all | solution.py:73
  1574.6 123.1 %reduce-scatter.10.cloned.1.call-start = ((), (), s32[]{:S(2)}) async-start(), calls=%async_computation.27 | async-start | bytes 1966080 | tf_op jit(solution)/shard_map/reduce_scatter | solution.py:390
  1588.9 256.4 %all-gather.57.cloned.1.call-start = ((), (), s32[]{:S(2)}) async-start(), calls=%async_computation.48 | async-start | bytes 5898240 | tf_op jit(solution)/shard_map/all_gather | solution.py:71
  1589.6 140.5 %copy-start.196 = (s32[256,1]{0,1:T(1,128)}, s32[256,1]{0,1:T(1,128)S(1)}, u32[]{:S(2)}) copy-start(s32[256,1]{0,1:T(1,128)S(1)} %get-tuple-element.147) | copy-start | bytes 3076
  1704.6 21.5 collective-permute-start.2
  1730.1 482.8 %copy-start.163 = (f32[256,2]{0,1:T(2,128)}, f32[256,2]{0,1:T(2,128)S(1)}, u32[]{:S(2)}) copy-start(f32[256,2]{0,1:T(2,128)S(1)} %get-tuple-element.51) | copy-start | bytes 6148
  1976.0 108.3 %all-to-all-start.14 = ((bf16[4,4,16,12,768]{4,2,3,1,0:T(8,128)(2,1)}), bf16[4,4,16,12,768]{4,2,3,1,0:T(8,128)(2,1)}, u32[]{:S(2)}, u32[]{:S(2)}) async-start(bf16[4,4,16,12,768]{4,2,3,1,0:T(8,128)(2,1)} %copy.319), calls=%async_computation.16 | async-start | bytes 9437184 | tf_op jit(solution)/shard_map/all_to_all | solution.py:73
  1981.0 183.4 %reduce-scatter.16.cloned.1.call-start = ((), (), s32[]{:S(2)}) async-start(), calls=%async_computation.30 | async-start | bytes 1966080 | tf_op jit(solution)/shard_map/reduce_scatter | solution.py:396
  2131.1 70.4 %reduce-scatter.14.cloned.1.call-start = ((), (), s32[]{:S(2)}) async-start(), calls=%async_computation.29 | async-start | bytes 1966080 | tf_op jit(solution)/shard_map/reduce_scatter | solution.py:390
  2145.5 179.0 %all-gather.59.cloned.1.call-start = ((), (), s32[]{:S(2)}) async-start(), calls=%async_computation.49 | async-start | bytes 5898240 | tf_op jit(solution)/shard_map/all_gather | solution.py:71
  2208.4 1.9 collective-permute-start.3
  2398.4 58.3 %all-to-all-start.16 = ((bf16[4,4,16,12,768]{4,2,3,0,1:T(8,128)(2,1)}), bf16[4,4,16,12,768]{4,2,3,0,1:T(8,128)(2,1)}, u32[]{:S(2)}, u32[]{:S(2)}) async-start(bf16[4,4,16,12,768]{4,2,3,0,1:T(8,128)(2,1)} %copy.330), calls=%async_computation.20 | async-start | bytes 9437184 | tf_op jit(solution)/shard_map/all_to_all | solution.py:74
  2461.6 219.5 %all-to-all-start.17 = ((bf16[4,4,16,12,768]{4,2,3,1,0:T(8,128)(2,1)}), bf16[4,4,16,12,768]{4,2,3,1,0:T(8,128)(2,1)}, u32[]{:S(2)}, u32[]{:S(2)}) async-start(bf16[4,4,16,12,768]{4,2,3,1,0:T(8,128)(2,1)} %copy.331), calls=%async_computation.21 | async-start | bytes 9437184 | tf_op jit(solution)/shard_map/all_to_all | solution.py:73
  2466.5 538.3 %reduce-scatter.20.cloned.1.call-start = ((), (), s32[]{:S(2)}) async-start(), calls=%async_computation.32 | async-start | bytes 1966080 | tf_op jit(solution)/shard_map/reduce_scatter | solution.py:396
  2720.5 284.3 %reduce-scatter.18.cloned.1.call-start = ((), (), s32[]{:S(2)}) async-start(), calls=%async_computation.31 | async-start | bytes 1966080 | tf_op jit(solution)/shard_map/reduce_scatter | solution.py:390
  2747.1 646.0 %reduce-scatter.26.cloned.1.call-start = ((), (), s32[]{:S(2)}) async-start(), calls=%async_computation.35 | async-start | bytes 417792 | tf_op jit(solution)/shard_map/reduce_scatter | solution.py:450
  2773.5 619.7 %reduce-scatter.24.cloned.1.call-start = ((), (), s32[]{:S(2)}) async-start(), calls=%async_computation.34 | async-start | bytes 2506752 | tf_op jit(solution)/shard_map/reduce_scatter | solution.py:449
  2778.0 615.2 %reduce-scatter.22.cloned.1.call-start = ((), (), s32[]{:S(2)}) async-start(), calls=%async_computation.33 | async-start | bytes 7520256 | tf_op jit(solution)/shard_map/reduce_scatter | solution.py:448
  (239 other events, 3363.9 us)
Sparse Core Ops, SparseCore 0:
  10.8 74.2 all-gather.32
  90.3 35.6 all-gather.36
  128.1 35.9 all-gather.34
  166.7 55.1 all-gather.38
  325.5 88.5 all-gather.40
  677.3 34.0 all-gather.44
  713.5 35.9 all-gather.42
  780.9 87.0 all-gather.46
  1103.8 35.0 all-gather.48
  1140.3 35.9 all-gather.50
  1177.8 88.2 all-gather.54
  1267.5 87.8 all-gather.52
  1555.4 64.1 reduce-scatter.11
  1621.8 75.8 reduce-scatter.9
  1758.4 86.8 all-gather.56
  2131.2 33.2 reduce-scatter.15
  2167.2 34.2 reduce-scatter.13
  2237.5 86.9 all-gather.58
  2720.6 35.5 reduce-scatter.19
  2758.3 34.2 reduce-scatter.17
  2797.8 120.4 reduce-scatter.25
  2924.6 126.5 reduce-scatter.23
  3057.1 150.5 reduce-scatter.21
where the time goes:
time: 3440 us; the launch traced here: 3400 us
  waiting for transfers between devices  976 us (28%)
  local copies, waits for them, and re-layouts  893 us (26%)
  matrix products  611 us (18%)
  blocking collectives  597 us (17%)
  other arithmetic  261 us (8%)
  starting transfers between devices  42.8 us (1%)
    rev x4, local copies, waits for them, and re-layouts, bias_rows(): return jnp.flip(tiled[:, :, :length], axis=2)  404 us
    all_gather x6, waiting for transfers between devices, expert_trip(): gathered = lax.all_gather(arrived[None], 'col', axis=0, tiled=True)  392 us
    all_to_all x6, waiting for transfers between devices, expert_trip(): lax.all_to_all(lax.all_to_all(partial_value.astype(jnp.bfloat16), 'row',...  270 us
    all_to_all x4, blocking collectives, expert_trip(): lax.all_to_all(partial_value.astype(jnp.bfloat16), 'row', split_axis=1, c...  228 us
    all_gather x1, blocking collectives, on_device(): lax.all_gather(router_weight[0], ('row', 'col'), axis=0, tiled=True)  134 us
    unnamed x2, blocking collectives  121 us
    reshape x4, local copies, waits for them, and re-layouts, bias_rows(): jnp.broadcast_to(diagonal[:, None, :], (HEADS, queries, queries + length...  120 us
    reduce_scatter x3, waiting for transfers between devices, on_device(): lax.psum_scatter(grad_keys.reshape(sequences, length, model_width).astype...  115 us
  transfers between devices with their start and end apart: 35, of which 23 were waited for; matrix products, arithmetic and copies ran while one was open for 39% of the time, Pallas kernels for 0%

commit v1 on v0

v1 whole, which is shorter than its diff:
```python
import functools

import jax
import jax.numpy as jnp
from jax import lax
from jax.experimental import pallas as pl
from jax.experimental.pallas import tpu as pltpu
from jax.sharding import PartitionSpec as P

HEADS = 12
HEAD_DIM = 64
EXPERTS = 64
TOP = 2
NBUCKET = 32
LANES = 128

EPS = 1e-06
MASKED = -1e30
HIGH = lax.Precision.HIGHEST
BF = jnp.bfloat16
F32 = jnp.float32
VMEM_LIMIT = 56 * 1024 * 1024
SCORE_ROWS = 16
SMALL_ROWS = 16
GELU_C = 0.7978845608028654
GELU_A = 0.044715


def norm_scale(stream, norm_gain):
    return stream * lax.rsqrt(jnp.mean(stream * stream, axis=-1, keepdims=True) + EPS) * norm_gain


X_PAIRS = [(i, i ^ 1) for i in range(4)]
Y_PAIRS = [(i, i ^ 2) for i in range(4)]


def swap_pipe(value):
    return lax.ppermute(value, "pipe", [(0, 1), (1, 0)])


def shift_col(value, distance):
    count = lax.axis_size("col")
    return lax.ppermute(value, "col", [(i, (i + distance) % count) for i in range(count)])


def is_small(rows, cols):
    return rows == 4 and cols == 4


def block_order(rows, cols):
    row, col = lax.axis_index("row"), lax.axis_index("col")
    if not is_small(rows, cols):
        return jnp.arange(rows * cols, dtype=jnp.int32)
    steps = jnp.arange(cols, dtype=jnp.int32)
    flips = jnp.arange(rows, dtype=jnp.int32)
    source_col = (col - steps + cols) % cols
    source_row = row ^ flips
    return (source_row[None, :] * cols + source_col[:, None]).reshape(-1)


def gather_groups(block):
    cols = lax.axis_size("col")
    half = block.shape[1] // 2
    groups = []
    for step in range(cols):
        following = shift_col(block, 1) if step + 1 < cols else None
        from_x = lax.ppermute(block, "row", X_PAIRS)
        from_y = lax.ppermute(block, "row", Y_PAIRS)
        left = lax.ppermute(from_y[:, :half], "row", X_PAIRS)
        right = lax.ppermute(from_x[:, half:], "row", Y_PAIRS)
        groups.append((block, from_x, from_y, left, right))
        block = following
    return groups


def scatter_groups(groups):
    cols = lax.axis_size("col")
    total = None
    for step in range(cols - 1, -1, -1):
        own, for_x, for_y, left, right = groups[step]
        half = left.shape[1]
        left = lax.ppermute(left, "row", X_PAIRS)
        right = lax.ppermute(right, "row", Y_PAIRS)
        for_y = jnp.concatenate(
            [(for_y[:, :half].astype(F32) + left.astype(F32)).astype(BF), for_y[:, half:]], axis=1
        )
        for_x = jnp.concatenate(
            [for_x[:, :half], (for_x[:, half:].astype(F32) + right.astype(F32)).astype(BF)], axis=1
        )
        from_x = lax.ppermute(for_x, "row", X_PAIRS)
        from_y = lax.ppermute(for_y, "row", Y_PAIRS)
        summed = own.astype(F32) + from_x.astype(F32) + from_y.astype(F32)
        if step:
            summed = shift_col(summed.astype(BF), cols - step).astype(F32)
        total = summed if total is None else total + summed
    return total


def gather_absolute(block, order):
    rows, cols = lax.axis_size("row"), lax.axis_size("col")
    if not is_small(rows, cols):
        return lax.all_gather(block, ("row", "col"), axis=0)
    whole = jnp.zeros((rows * cols,) + block.shape, block.dtype)
    for step, (own, from_x, from_y, left, right) in enumerate(gather_groups(block)):
        across = jnp.concatenate([left, right], axis=1)
        for flip, value in enumerate((own, from_x, from_y, across)):
            whole = lax.dynamic_update_index_in_dim(whole, value, order[step * rows + flip], 0)
    return whole


def gather_tokens(block):
    if is_small(lax.axis_size("row"), lax.axis_size("col")):
        return gather_groups(block)
    return lax.all_gather(block, ("row", "col"), axis=0)


def scatter_tokens(parts):
    if is_small(lax.axis_size("row"), lax.axis_size("col")):
        return scatter_groups(parts)
    return lax.psum_scatter(parts, ("row", "col"), scatter_dimension=0, tiled=False).astype(F32)


def scatter_absolute(parts, order):
    rows, cols = lax.axis_size("row"), lax.axis_size("col")
    if not is_small(rows, cols):
        return lax.psum_scatter(parts, ("row", "col"), scatter_dimension=0, tiled=False).astype(F32)
    half = parts.shape[2] // 2
    groups = []
    for step in range(cols):
        own, for_x, for_y, across = [
            lax.dynamic_index_in_dim(parts, order[step * rows + flip], 0, keepdims=False)
            for flip in range(rows)
        ]
        groups.append((own, for_x, for_y, across[:, :half], across[:, half:]))
    return scatter_groups(groups)


def gather_sequence(block):
    rows, cols = lax.axis_size("row"), lax.axis_size("col")
    if not is_small(rows, cols):
        return lax.all_gather(block, "col", axis=0, tiled=True)
    col = lax.axis_index("col")
    count = block.shape[0]
    whole = jnp.zeros((cols * count, block.shape[1]), block.dtype)
    for step in range(cols):
        place = (col - step + cols) % cols * count
        whole = lax.dynamic_update_slice(whole, block, (place, jnp.zeros_like(place)))
        if step + 1 < cols:
            block = shift_col(block, 1)
    return whole


def scatter_sequence(parts):
    rows, cols = lax.axis_size("row"), lax.axis_size("col")
    if not is_small(rows, cols):
        return lax.psum_scatter(parts, "col", scatter_dimension=0, tiled=True).astype(F32)
    col = lax.axis_index("col")
    count = parts.shape[0] // cols
    total = None
    for step in range(cols):
        place = (col - step + cols) % cols * count
        piece = lax.dynamic_slice_in_dim(parts, place, count, 0)
        if step:
            piece = shift_col(piece, cols - step)
        total = piece.astype(F32) if total is None else total + piece.astype(F32)
    return total


def score_tile(query, key, diagonal, mask):
    tokens, length = query.shape[0], key.shape[0]
    width = diagonal.shape[-1]
    spread = jnp.broadcast_to(diagonal, (tokens, width))
    bias = pltpu.roll(spread, 0, 1, stride=1, stride_axis=0)[:, :length]
    raw = lax.dot_general(query, key, (((1,), (1,)), ((), ())), preferred_element_type=F32)
    return raw + bias + mask


def attention_fwd_kernel(q_ref, k_ref, v_ref, diag_ref, mask_ref, out_ref, lse_ref):
    mask = mask_ref[...]
    for sub in range(2):
        lanes = slice(sub * HEAD_DIM, (sub + 1) * HEAD_DIM)
        scores = score_tile(
            q_ref[:, lanes] * BF(HEAD_DIM**-0.5), k_ref[:, lanes], diag_ref[0, sub : sub + 1], mask
        )
        maxima = jnp.max(scores, axis=-1, keepdims=True)
        weights = jnp.exp(scores - maxima)
        totals = jnp.sum(weights, axis=-1, keepdims=True)
        probability = (weights * (1.0 / totals)).astype(BF)
        out = jnp.dot(probability, v_ref[:, lanes], preferred_element_type=F32)
        out_ref[:, lanes] = out.astype(BF)
        lse_ref[:, lanes] = jnp.broadcast_to(maxima + jnp.log(totals), out.shape)


def attention_forward(q, key, value, diagonals, mask):
    tokens, width = q.shape
    length = key.shape[0]
    pairs = width // LANES
    return pl.pallas_call(
        attention_fwd_kernel,
        grid=(pairs,),
        in_specs=[
            pl.BlockSpec((tokens, LANES), lambda i: (0, i)),
            pl.BlockSpec((length, LANES), lambda i: (0, i)),
            pl.BlockSpec((length, LANES), lambda i: (0, i)),
            pl.BlockSpec((1, 2, diagonals.shape[-1]), lambda i: (i, 0, 0)),
            pl.BlockSpec((tokens, length), lambda i: (0, 0)),
        ],
        out_specs=[
            pl.BlockSpec((tokens, LANES), lambda i: (0, i)),
            pl.BlockSpec((tokens, LANES), lambda i: (0, i)),
        ],
        out_shape=[
            jax.ShapeDtypeStruct((tokens, width), BF),
            jax.ShapeDtypeStruct((tokens, width), F32),
        ],
        compiler_params=pltpu.CompilerParams(vmem_limit_bytes=VMEM_LIMIT),
        cost_estimate=pl.CostEstimate(
            flops=4 * tokens * length * width,
            bytes_accessed=8 * length * width,
            transcendentals=HEADS * tokens * length,
        ),
        name="attention_forward",
    )(q, key, value, diagonals, mask)


def attention_bwd_kernel(
    q_ref, k_ref, v_ref, ga_ref, lse_ref, diag_ref, mask_ref, dq_ref, dk_ref, dv_ref, dist_ref
):
    mask = mask_ref[...]
    tokens, length = mask.shape
    width = diag_ref.shape[-1]
    for sub in range(2):
        lanes = slice(sub * HEAD_DIM, (sub + 1) * HEAD_DIM)
        query = q_ref[:, lanes] * BF(HEAD_DIM**-0.5)
        key = k_ref[:, lanes]
        grad = ga_ref[:, lanes]
        scores = score_tile(query, key, diag_ref[0, sub : sub + 1], mask)
        lse = lse_ref[:, sub * HEAD_DIM : sub * HEAD_DIM + 1]
        probability = jnp.exp(scores - lse)
        dv = lax.dot_general(
            probability.astype(BF), grad, (((0,), (0,)), ((), ())), preferred_element_type=F32
        )
        dv_ref[:, lanes] = dv.astype(BF)
        grad_prob = lax.dot_general(
            grad, v_ref[:, lanes], (((1,), (1,)), ((), ())), preferred_element_type=F32
        )
        product = probability * grad_prob
        inner = jnp.sum(product, axis=-1, keepdims=True)
        grad_scores = product - probability * inner
        low = grad_scores.astype(BF)
        dq = jnp.dot(low, key, preferred_element_type=F32) * HEAD_DIM**-0.5
        dq_ref[:, lanes] = dq.astype(BF)
        dk = lax.dot_general(low, query, (((0,), (0,)), ((), ())), preferred_element_type=F32)
        dk_ref[:, lanes] = dk.astype(BF)
        turned = jnp.concatenate(
            [grad_scores, jnp.zeros((tokens, width - length), F32)], axis=1
        )
        half = tokens // 2
        while half >= 8:
            turned = turned[:half] + pltpu.roll(turned[half:], width - half, 1)
            half //= 2
        dist_ref[0, sub] = turned


def attention_backward(q, key, value, grad, lse, diagonals, mask):
    tokens, width = q.shape
    length = key.shape[0]
    pairs = width // LANES
    wide = diagonals.shape[-1]
    return pl.pallas_call(
        attention_bwd_kernel,
        grid=(pairs,),
        in_specs=[
            pl.BlockSpec((tokens, LANES), lambda i: (0, i)),
            pl.BlockSpec((length, LANES), lambda i: (0, i)),
            pl.BlockSpec((length, LANES), lambda i: (0, i)),
            pl.BlockSpec((tokens, LANES), lambda i: (0, i)),
            pl.BlockSpec((tokens, LANES), lambda i: (0, i)),
            pl.BlockSpec((1, 2, wide), lambda i: (i, 0, 0)),
            pl.BlockSpec((tokens, length), lambda i: (0, 0)),
        ],
        out_specs=[
            pl.BlockSpec((tokens, LANES), lambda i: (0, i)),
            pl.BlockSpec((length, LANES), lambda i: (0, i)),
            pl.BlockSpec((length, LANES), lambda i: (0, i)),
            pl.BlockSpec((1, 2, 8, wide), lambda i: (i, 0, 0, 0)),
        ],
        out_shape=[
            jax.ShapeDtypeStruct((tokens, width), BF),
            jax.ShapeDtypeStruct((length, width), BF),
            jax.ShapeDtypeStruct((length, width), BF),
            jax.ShapeDtypeStruct((pairs, 2, 8, wide), F32),
        ],
        compiler_params=pltpu.CompilerParams(vmem_limit_bytes=VMEM_LIMIT),
        cost_estimate=pl.CostEstimate(
            flops=10 * tokens * length * width,
            bytes_accessed=12 * length * width,
            transcendentals=HEADS * tokens * length,
        ),
        name="attention_backward",
    )(q, key, value, grad, lse, diagonals, mask)


def weight_copies(own, other, buffer, sem, expert, slot):
    return (
        pltpu.make_async_copy(own.at[expert], buffer.at[slot], sem.at[slot]),
        pltpu.make_async_copy(other.at[expert], buffer.at[slot], sem.at[slot]),
    )


def start_weights(own_flag, refs, expert, slot):
    for own, other, buffer, sem in refs:

        @pl.when(own_flag)
        def _():
            weight_copies(own, other, buffer, sem, expert, slot)[0].start()

        @pl.when(jnp.logical_not(own_flag))
        def _():
            weight_copies(own, other, buffer, sem, expert, slot)[1].start()


def wait_weights(refs, expert, slot):
    for own, _, buffer, sem in refs:
        pltpu.make_async_copy(own.at[expert], buffer.at[slot], sem.at[slot]).wait()


def split_two(value):
    high = value.astype(BF)
    return high, (value - high.astype(F32)).astype(BF)


def buffer_places(buffer, slot):
    half = buffer.shape[-1] // 2
    return (
        buffer.at[slot, 0],
        buffer.at[slot, 1],
        buffer.at[slot, 2],
        buffer.at[slot, 3, :, pl.ds(0, half)],
        buffer.at[slot, 3, :, pl.ds(half, half)],
    )


class Feed:
    def __init__(self, value):
        self.grouped = isinstance(value, list)
        self.arrays = [part for group in value for part in group] if self.grouped else [value]
        self.tokens, self.width = self.arrays[0].shape[-2:]

    def specs(self, group, index_map):
        if self.grouped:
            return [pl.BlockSpec(memory_space=pl.ANY)] * len(self.arrays)
        return [pl.BlockSpec((group, self.tokens, self.width), index_map)]

    def scratch(self):
        if not self.grouped:
            return []
        return [pltpu.VMEM((2, 4, self.tokens, self.width), BF), pltpu.SemaphoreType.DMA((2, 5))]


def feed_copies(refs, scratch, step, slot):
    buffer, sem = scratch
    return [
        pltpu.make_async_copy(refs[5 * step + k], place, sem.at[slot, k])
        for k, place in enumerate(buffer_places(buffer, slot))
    ]


def start_feed(refs, scratch, step, slot):
    for at in range(len(refs) // 5):

        @pl.when(step == at)
        def _():
            for copy in feed_copies(refs, scratch, at, slot):
                copy.start()


def take_feed(refs, scratch, step):
    if not scratch:
        return [refs[0][g] for g in range(refs[0].shape[0])]
    slot = lax.rem(step, 2)
    for copy in feed_copies(refs, scratch, 0, slot):
        copy.wait()
    return [scratch[0][slot, g] for g in range(4)]


def refill_feed(refs, scratch, step):
    if scratch:
        start_feed(refs, scratch, step + 2, lax.rem(step, 2))


def open_feed(refs, scratch):
    if scratch:
        start_feed(refs, scratch, 0, 0)
        start_feed(refs, scratch, 1, 1)


def sink_copies(refs, scratch, step, slot):
    buffer, sem = scratch
    return [
        pltpu.make_async_copy(place, refs[5 * step + k], sem.at[slot, k])
        for k, place in enumerate(buffer_places(buffer, slot))
    ]


def put_sink(refs, scratch, step, values):
    if not scratch:
        for g, value in enumerate(values):
            refs[0][g] = value
        return
    slot = lax.rem(step, 2)

    @pl.when(step >= 2)
    def _():
        for copy in sink_copies(refs, scratch, 0, slot):
            copy.wait()

    for g, value in enumerate(values):
        scratch[0][slot, g] = value
    for at in range(len(refs) // 5):

        @pl.when(step == at)
        def _():
            for copy in sink_copies(refs, scratch, at, slot):
                copy.start()


def close_sink(refs, scratch, steps):
    if scratch:
        for step in range(max(steps - 2, 0), steps):
            for copy in sink_copies(refs, scratch, 0, step % 2):
                copy.wait()


def sink_specs(grouped, blocks, group, rows, width, index_map):
    if not grouped:
        return (
            [pl.BlockSpec((group, rows, width), index_map)],
            [jax.ShapeDtypeStruct((blocks, rows, width), BF)],
            [],
        )
    shapes = []
    for _ in range(blocks // 4):
        shapes += [jax.ShapeDtypeStruct((rows, width), BF)] * 3
        shapes += [jax.ShapeDtypeStruct((rows, width // 2), BF)] * 2
    return (
        [pl.BlockSpec(memory_space=pl.ANY)] * len(shapes),
        shapes,
        [pltpu.VMEM((2, 4, rows, width), BF), pltpu.SemaphoreType.DMA((2, 5))],
    )


def regroup(values):
    return [tuple(values[5 * k : 5 * k + 5]) for k in range(len(values) // 5)] if len(values) > 1 else values[0]


def spread_slots(table, rows):
    return lax.dot_general(table, rows, (((0,), (0,)), ((), ())), preferred_element_type=F32)


def expert_fwd_kernel(section, group, steps, experts, counts, *refs):
    n_feed, n_sink, n_feed_scratch, n_sink_scratch = counts
    pipe_ref, refs = refs[0], refs[1:]
    feed, refs = refs[:n_feed], refs[n_feed:]
    tab_ref, named_ref, pick_ref, router_ref, own_in, oth_in, own_out, oth_out = refs[:8]
    refs = refs[8:]
    sink, refs = refs[:n_sink], refs[n_sink:]
    rows_ref, gate_ref, held, gates, buf_in, buf_out, sem_in, sem_out = refs[:8]
    refs = refs[8:]
    feed_scratch, sink_scratch = refs[:n_feed_scratch], refs[n_feed_scratch:]
    i = pl.program_id(0)
    own_flag = pipe_ref[0] == section
    weights = ((own_in, oth_in, buf_in, sem_in), (own_out, oth_out, buf_out, sem_out))
    blocks, local, places, width = held.shape
    slots = local * places

    @pl.when(i == 0)
    def _():
        open_feed(feed, feed_scratch)
        start_weights(own_flag, weights, 0, 0)
        if experts > 1:
            start_weights(own_flag, weights, 1, 1)

    @pl.when(i < steps)
    def _():
        values = take_feed(feed, feed_scratch, i)
        for g, tokens in enumerate(values):
            table = tab_ref[g]
            logits = jnp.dot(tokens, router_ref[...], preferred_element_type=F32)
            logits = jnp.where(named_ref[g].astype(F32) > 0, logits, MASKED)
            chosen = jnp.exp(logits - jnp.max(logits, axis=-1, keepdims=True))
            chosen = chosen / jnp.sum(chosen, axis=-1, keepdims=True)
            high, low = split_two(chosen)
            spread = jnp.dot(
                table, jnp.concatenate([high, low], axis=1), preferred_element_type=F32
            )
            spread = (spread[:, :LANES] + spread[:, LANES:]) * pick_ref[...]
            gate = jnp.broadcast_to(jnp.sum(spread, axis=-1, keepdims=True), (slots, LANES))
            rows = jnp.dot(table, tokens, preferred_element_type=F32).astype(BF)
            rows_ref[g] = rows.reshape(local, places, width)
            gate_ref[g] = gate.reshape(local, places, LANES)
            held[i * group + g] = rows.reshape(local, places, width)
            gates[i * group + g] = gate.reshape(local, places, LANES)
        refill_feed(feed, feed_scratch, i)

    @pl.when((i >= steps) & (i < steps + experts))
    def _():
        expert = i - steps
        slot = lax.rem(expert, 2)
        wait_weights(weights, expert, slot)
        part = blocks // 2 if blocks % 2 == 0 else blocks
        for start in range(0, blocks, part):
            some = pl.ds(start, part)
            rows = held[some, expert].reshape(part * places, width)
            hidden = jnp.dot(rows, buf_in[slot], preferred_element_type=F32)
            bent = jnp.tanh(GELU_C * (hidden + GELU_A * hidden * hidden * hidden))
            active = (0.5 * hidden * (1.0 + bent)).astype(BF)
            result = jnp.dot(active, buf_out[slot], preferred_element_type=F32)
            gate = gates[some, expert].reshape(part * places, LANES)[:, :1]
            held[some, expert] = (result * gate).astype(BF).reshape(part, places, width)

        @pl.when(expert + 2 < experts)
        def _():
            start_weights(own_flag, weights, expert + 2, slot)

    @pl.when(i >= steps + experts)
    def _():
        step = i - steps - experts
        values = [
            spread_slots(tab_ref[g], held[step * group + g].reshape(slots, width)).astype(BF)
            for g in range(group)
        ]
        put_sink(sink, sink_scratch, step, values)

    @pl.when(i == 2 * steps + experts - 1)
    def _():
        close_sink(sink, sink_scratch, steps)


def group_of(blocks):
    return 4 if blocks % 4 == 0 else 1


def grid_maps(steps, experts):
    def early(i, *_):
        return (jnp.minimum(i, steps - 1), 0, 0)

    def early4(i, *_):
        return (jnp.minimum(i, steps - 1), 0, 0, 0)

    def both(i, *_):
        return (jnp.where(i < steps + experts, jnp.minimum(i, steps - 1), i - steps - experts), 0, 0)

    def late(i, *_):
        return (jnp.maximum(i - steps - experts, 0), 0, 0)

    def per_expert(i, *_):
        return (0, jnp.clip(i - steps, 0, experts - 1), 0, 0)

    return early, early4, both, late, per_expert


def expert_forward(section, pipe, tables, tokens, named, pick, router, weights):
    own_in, oth_in, own_out, oth_out = weights
    blocks, slots, count = tables.shape
    feed = Feed(tokens)
    width = feed.width
    experts, _, hidden = own_in.shape
    places = slots // experts
    group = group_of(blocks)
    steps = blocks // group
    early, early4, both, late, _ = grid_maps(steps, experts)
    any_spec = pl.BlockSpec(memory_space=pl.ANY)
    sink_out, sink_shapes, sink_scratch = sink_specs(feed.grouped, blocks, group, count, width, late)
    feed_scratch = feed.scratch()
    counts = (len(feed.arrays), len(sink_out), len(feed_scratch), len(sink_scratch))
    *parts, rows, gates = pl.pallas_call(
        functools.partial(expert_fwd_kernel, section, group, steps, experts, counts),
        grid_spec=pltpu.PrefetchScalarGridSpec(
            num_scalar_prefetch=1,
            grid=(2 * steps + experts,),
            in_specs=feed.specs(group, early)
            + [
                pl.BlockSpec((group, slots, count), both),
                pl.BlockSpec((group, count, LANES), early),
                pl.BlockSpec((slots, LANES), lambda i, *_: (0, 0)),
                pl.BlockSpec((width, LANES), lambda i, *_: (0, 0)),
            ]
            + [any_spec] * 4,
            out_specs=sink_out
            + [
                pl.BlockSpec((group, experts, places, width), early4),
                pl.BlockSpec((group, experts, places, LANES), early4),
            ],
            scratch_shapes=[
                pltpu.VMEM((blocks, experts, places, width), BF),
                pltpu.VMEM((blocks, experts, places, LANES), F32),
                pltpu.VMEM((2, width, hidden), BF),
                pltpu.VMEM((2, hidden, width), BF),
                pltpu.SemaphoreType.DMA((2,)),
                pltpu.SemaphoreType.DMA((2,)),
            ]
            + feed_scratch
            + sink_scratch,
        ),
        out_shape=sink_shapes
        + [
            jax.ShapeDtypeStruct((blocks, experts, places, width), BF),
            jax.ShapeDtypeStruct((blocks, experts, places, LANES), F32),
        ],
        compiler_params=pltpu.CompilerParams(vmem_limit_bytes=VMEM_LIMIT),
        cost_estimate=pl.CostEstimate(
            flops=4 * blocks * slots * width * hidden,
            bytes_accessed=4 * experts * width * hidden + 8 * blocks * count * width,
            transcendentals=blocks * slots * hidden,
        ),
        name="expert_forward",
    )(pipe, *feed.arrays, tables, named, pick, router, own_in, oth_in, own_out, oth_out)
    return regroup(parts), rows, gates


def expert_bwd_kernel(section, group, steps, experts, counts, *refs):
    n_feed, n_sink, n_feed_scratch, n_sink_scratch, n_alias = counts
    pipe_ref, refs = refs[0], refs[1:]
    feed, refs = refs[:n_feed], refs[n_feed:]
    tab_ref, rows_ref, gate_ref, lane_ref, own_in, oth_in, own_out, oth_out = refs[:8]
    refs = refs[8 + n_alias :]
    sink, refs = refs[:n_sink], refs[n_sink:]
    kept_in, kept_out, sent_in, sent_out = refs[:4]
    refs = refs[4:]
    held, marks, buf_in, buf_out, grad_in, grad_out, sem_in, sem_out, sem_grad = refs[:9]
    refs = refs[9:]
    feed_scratch, sink_scratch = refs[:n_feed_scratch], refs[n_feed_scratch:]
    i = pl.program_id(0)
    own_flag = pipe_ref[0] == section
    weights = ((own_in, oth_in, buf_in, sem_in), (own_out, oth_out, buf_out, sem_out))
    blocks, local, places, width = held.shape
    slots = local * places

    def grad_copies(keep, expert, slot):
        target_in, target_out = (kept_in, kept_out) if keep else (sent_in, sent_out)
        return (
            pltpu.make_async_copy(grad_in.at[slot], target_in.at[expert], sem_grad.at[0, slot]),
            pltpu.make_async_copy(grad_out.at[slot], target_out.at[expert], sem_grad.at[1, slot]),
        )

    def wait_grads(expert, slot):
        for copy in grad_copies(True, expert, slot):
            copy.wait()

    @pl.when(i == 0)
    def _():
        open_feed(feed, feed_scratch)
        start_weights(own_flag, weights, 0, 0)
        if experts > 1:
            start_weights(own_flag, weights, 1, 1)

    @pl.when(i < steps)
    def _():
        for g, tokens in enumerate(take_feed(feed, feed_scratch, i)):
            rows = jnp.dot(tab_ref[g], tokens, preferred_element_type=F32).astype(BF)
            held[i * group + g] = rows.reshape(local, places, width)
        refill_feed(feed, feed_scratch, i)

    @pl.when((i >= steps) & (i < steps + experts))
    def _():
        expert = i - steps
        slot = lax.rem(expert, 2)
        count = blocks * places
        wait_weights(weights, expert, slot)

        @pl.when(expert >= 2)
        def _():
            wait_grads(expert, slot)

        rows = rows_ref[...].reshape(count, width)
        gate = gate_ref[...].reshape(count, LANES)[:, :1]
        grad = held[:, expert].reshape(count, width)
        hidden = jnp.dot(rows, buf_in[slot], preferred_element_type=F32)
        square = hidden * hidden
        bent = jnp.tanh(GELU_C * (hidden + GELU_A * square * hidden))
        active = (0.5 * hidden * (1.0 + bent)).astype(BF)
        slope = 0.5 * (1.0 + bent) + (0.5 * GELU_C) * hidden * (1.0 - bent * bent) * (
            1.0 + (3.0 * GELU_A) * square
        )
        grad_act = lax.dot_general(
            grad, buf_out[slot], (((1,), (1,)), ((), ())), preferred_element_type=F32
        )
        mark = jnp.sum(active.astype(F32) * grad_act, axis=-1, keepdims=True)
        first = mark.astype(BF).astype(F32)
        lanes = lane_ref[...].reshape(count, LANES).astype(F32)
        which = lax.rem(lax.broadcasted_iota(jnp.int32, (count, LANES), 1), 8)
        value = jnp.where(which == 0, first, mark - first)
        marks[:, expert] = (value * lanes).astype(BF).reshape(blocks, places, LANES)
        gated = (grad.astype(F32) * gate).astype(BF)
        grad_out[slot] = spread_slots(active, gated).astype(BF)
        grad_hidden = (grad_act * gate * slope).astype(BF)
        grad_in[slot] = spread_slots(rows, grad_hidden).astype(BF)
        back = lax.dot_general(
            grad_hidden, buf_in[slot], (((1,), (1,)), ((), ())), preferred_element_type=F32
        )
        held[:, expert] = back.astype(BF).reshape(blocks, places, width)

        @pl.when(own_flag)
        def _():
            for copy in grad_copies(True, expert, slot):
                copy.start()

        @pl.when(jnp.logical_not(own_flag))
        def _():
            for copy in grad_copies(False, expert, slot):
                copy.start()

        @pl.when(expert + 2 < experts)
        def _():
            start_weights(own_flag, weights, expert + 2, slot)

    @pl.when(i >= steps + experts)
    def _():
        step = i - steps - experts
        values = []
        for g in range(group):
            place = step * group + g
            table = tab_ref[g]
            rows = spread_slots(table, held[place].reshape(slots, width))
            found = spread_slots(marks[place].reshape(slots, LANES), table)
            count = found.shape[1]
            line = jnp.concatenate(
                [
                    jnp.sum(found[0:8], axis=0, keepdims=True),
                    jnp.sum(found[8:16], axis=0, keepdims=True),
                    jnp.zeros((1, width - 2 * count), F32),
                ],
                axis=1,
            )
            values.append(
                jnp.concatenate(
                    [rows.astype(BF), jnp.broadcast_to(line, (SCORE_ROWS, width)).astype(BF)], axis=0
                )
            )
        put_sink(sink, sink_scratch, step, values)

    @pl.when(i == 2 * steps + experts - 1)
    def _():
        close_sink(sink, sink_scratch, steps)
        for expert in range(max(experts - 2, 0), experts):
            wait_grads(expert, expert % 2)


def expert_backward(section, pipe, tables, grads, rows, gates, lanes, weights, stores):
    own_in, oth_in, own_out, oth_out = weights
    blocks, slots, count = tables.shape
    feed = Feed(grads)
    width = feed.width
    experts, _, hidden = own_in.shape
    places = slots // experts
    group = group_of(blocks)
    steps = blocks // group
    early, _, both, late, per_expert = grid_maps(steps, experts)
    any_spec = pl.BlockSpec(memory_space=pl.ANY)
    sink_out, sink_shapes, sink_scratch = sink_specs(
        feed.grouped, blocks, group, count + SCORE_ROWS, width, late
    )
    feed_scratch = feed.scratch()
    shape_in = jax.ShapeDtypeStruct(own_in.shape, BF)
    shape_out = jax.ShapeDtypeStruct(own_out.shape, BF)
    operands = [pipe, *feed.arrays, tables, rows, gates, lanes, own_in, oth_in, own_out, oth_out]
    aliases = {}
    if stores is not None:
        aliases = {len(operands) + k: len(sink_out) + k for k in range(4)}
        operands += list(stores)
    counts = (len(feed.arrays), len(sink_out), len(feed_scratch), len(sink_scratch), len(aliases))
    outs = pl.pallas_call(
        functools.partial(expert_bwd_kernel, section, group, steps, experts, counts),
        grid_spec=pltpu.PrefetchScalarGridSpec(
            num_scalar_prefetch=1,
            grid=(2 * steps + experts,),
            in_specs=feed.specs(group, early)
            + [
                pl.BlockSpec((group, slots, count), both),
                pl.BlockSpec((blocks, 1, places, width), per_expert),
                pl.BlockSpec((blocks, 1, places, LANES), per_expert),
                pl.BlockSpec((blocks, 1, places, LANES), per_expert),
            ]
            + [any_spec] * (4 + len(aliases)),
            out_specs=sink_out + [any_spec] * 4,
            scratch_shapes=[
                pltpu.VMEM((blocks, experts, places, width), BF),
                pltpu.VMEM((blocks, experts, places, LANES), BF),
                pltpu.VMEM((2, width, hidden), BF),
                pltpu.VMEM((2, hidden, width), BF),
                pltpu.VMEM((2, width, hidden), BF),
                pltpu.VMEM((2, hidden, width), BF),
                pltpu.SemaphoreType.DMA((2,)),
                pltpu.SemaphoreType.DMA((2,)),
                pltpu.SemaphoreType.DMA((2, 2)),
            ]
            + feed_scratch
            + sink_scratch,
        ),
        out_shape=sink_shapes + [shape_in, shape_out, shape_in, shape_out],
        input_output_aliases=aliases,
        compiler_params=pltpu.CompilerParams(vmem_limit_bytes=VMEM_LIMIT),
        cost_estimate=pl.CostEstimate(
            flops=10 * blocks * slots * width * hidden,
            bytes_accessed=8 * experts * width * hidden + 8 * blocks * count * width,
            transcendentals=blocks * slots * hidden,
        ),
        name="expert_backward",
    )(*operands)
    return regroup(outs[: len(sink_out)]), outs[len(sink_out) :]


def dense_kernel(normed_ref, seq_ref, att_ref, dq_ref, dk_ref, dv_ref, branch_ref, out_ref):
    quarter = pl.program_id(0) // 3

    def product(left, right):
        out_ref[...] = spread_slots(left[...], right[...]).astype(BF)

    pl.when(quarter == 0)(lambda: product(normed_ref, dq_ref))
    pl.when(quarter == 1)(lambda: product(seq_ref, dk_ref))
    pl.when(quarter == 2)(lambda: product(seq_ref, dv_ref))
    pl.when(quarter == 3)(lambda: product(att_ref, branch_ref))


def dense_grads(normed, sequence, attended, dq, dk, dv, branch):
    tokens, width = normed.shape
    length = sequence.shape[0]
    third = width // 3

    def whole(rows):
        return pl.BlockSpec((rows, width), lambda i: (0, 0))

    def block(rows, quarter):
        return pl.BlockSpec((rows, third), lambda i: (0, jnp.clip(i - 3 * quarter, 0, 2)))

    return pl.pallas_call(
        dense_kernel,
        grid=(12,),
        in_specs=[
            whole(tokens), whole(length), whole(tokens),
            block(tokens, 0), block(length, 1), block(length, 2), block(tokens, 3),
        ],
        out_specs=pl.BlockSpec((width, third), lambda i: (0, i)),
        out_shape=jax.ShapeDtypeStruct((width, 4 * width), BF),
        compiler_params=pltpu.CompilerParams(vmem_limit_bytes=VMEM_LIMIT),
        cost_estimate=pl.CostEstimate(
            flops=4 * width * width * (tokens + length),
            bytes_accessed=8 * length * width + 8 * width * width,
            transcendentals=0,
        ),
        name="dense_grads",
    )(normed, sequence, attended, dq, dk, dv, branch)


def slot_tables(named_by, first_expert, local_experts, places):
    tokens = named_by.shape[-1]
    ids = first_expert + jnp.arange(local_experts, dtype=jnp.int32)
    hot = [named_by[:, k, None, :] == ids[None, :, None] for k in range(TOP)]
    before = (
        jnp.arange(tokens, dtype=jnp.int32)[:, None] < jnp.arange(tokens, dtype=jnp.int32)[None, :]
    ).astype(BF)
    code = jnp.full(hot[0].shape, -1, jnp.int32)
    earlier = jnp.zeros(hot[0].shape[:2] + (1,), F32)
    for k in range(TOP):
        ones = hot[k].astype(BF)
        running = jnp.einsum("bet,tu->beu", ones, before, preferred_element_type=F32) + earlier
        code = jnp.where(hot[k], running.astype(jnp.int32), code)
        earlier = earlier + jnp.sum(ones.astype(F32), axis=-1, keepdims=True)
    place = jnp.arange(places, dtype=jnp.int32)
    equal = code[:, :, None, :] == place[None, None, :, None]
    tables = equal.astype(BF)
    second = jnp.max(jnp.where(equal & hot[1][:, :, None, :], 1.0, 0.0), axis=-1)
    lane = jnp.arange(LANES, dtype=jnp.int32)
    wanted = jnp.where(second[..., None] > 0.5, (lane >= 8) & (lane < 11), lane < 3)
    blocks = named_by.shape[0]
    return tables.reshape(blocks, local_experts * places, tokens), wanted.astype(BF)


def named_mask(named_by):
    lane = jnp.arange(LANES, dtype=jnp.int32)
    hit = named_by[:, 0, :, None] == lane
    for k in range(1, TOP):
        hit = hit | (named_by[:, k, :, None] == lane)
    return hit.astype(BF)


def on_device(
    section_input,
    cotangent,
    qkv_weight,
    out_weight,
    router_weight,
    gain_attn,
    gain_moe,
    rel_bias,
    expert_in,
    expert_out,
    routes,
    doc_ids,
    buckets,
):
    pipe = lax.axis_index("pipe")
    row, col = lax.axis_index("row"), lax.axis_index("col")
    row_count, col_count = lax.axis_size("row"), lax.axis_size("col")
    group_size = row_count * col_count
    tokens, width = section_input.shape[1:]
    length = buckets.shape[0]
    capacity = 3 * tokens * TOP // (2 * EXPERTS)
    places = -(-capacity // 16) * 16
    local_experts = expert_in.shape[1]
    first = pipe == 0
    pipe_word = pipe.astype(jnp.int32)[None]
    order = block_order(row_count, col_count)

    shard = qkv_weight.shape[1]
    bias_count = rel_bias.shape[1]
    middle = 2 * width

    def line(values):
        flat = jnp.concatenate([value.reshape(-1) for value in values])
        return jnp.pad(flat, (0, 2 * middle - flat.shape[0])).reshape(2, middle)

    small = jnp.concatenate(
        [
            line([router_weight[0]]),
            line([gain_attn[0], gain_moe[0], rel_bias[0]]),
            line([jnp.swapaxes(routes[0], 1, 2).astype(BF)]),
            jnp.zeros((SMALL_ROWS - 6, middle), BF),
        ],
        axis=0,
    )
    left = qkv_weight[0][:, :middle]
    right = jnp.concatenate([qkv_weight[0][:, middle:], out_weight[0]], axis=1)
    swapped = swap_pipe(jnp.where(first, right, left))
    mine = [jnp.where(first, left, swapped), jnp.where(first, swapped, right)]
    whole = gather_absolute(jnp.concatenate([mine[0], small], axis=0), order)
    whole = lax.optimization_barrier(whole)
    partner = swap_pipe(whole)
    later, _ = lax.optimization_barrier((mine[1], whole))
    later = lax.all_gather(later, ("row", "col"), axis=0)
    later_partner = swap_pipe(later)
    expert_first, expert_second, _ = lax.optimization_barrier((expert_in[0], expert_out[0], swapped))
    expert_weights = (expert_first, swap_pipe(expert_first), expert_second, swap_pipe(expert_second))
    halves = [
        [jnp.where(first, whole[:, :shard], partner[:, :shard]), jnp.where(first, partner[:, :shard], whole[:, :shard])],
        [jnp.where(first, later, later_partner), jnp.where(first, later_partner, later)],
    ]
    smalls = [
        jnp.where(first, whole[:, shard:], partner[:, shard:]),
        jnp.where(first, partner[:, shard:], whole[:, shard:]),
    ]
    params = []
    names = []
    for section in range(2):
        lines = smalls[section].reshape(group_size, SMALL_ROWS // 2, 2 * middle)
        low, high = [value.reshape(width, middle) for value in halves[section]]
        router = lines[:, 0, : shard * EXPERTS].reshape(width, EXPERTS)
        params.append(
            dict(
                q=low[:, :width],
                k=low[:, width:],
                v=high[:, :width],
                out=high[:, width:],
                router=jnp.pad(router, ((0, 0), (0, LANES - EXPERTS))),
                gain_attn=lines[:, 1, :shard].reshape(width).astype(F32),
                gain_moe=lines[:, 1, shard : 2 * shard].reshape(width).astype(F32),
                table=lines[:, 1, 2 * shard : 2 * shard + bias_count].reshape(NBUCKET, HEADS),
            )
        )
        named_by = lines[:, 2, : 2 * TOP * tokens].reshape(group_size, 2, TOP, tokens)
        named_by = lax.dynamic_index_in_dim(named_by, pipe, 1, keepdims=False)
        names.append(named_by.astype(jnp.int32))

    first_expert = row * local_experts
    tables, lane_masks, named = [], [], []
    for section in range(2):
        placed = jnp.take(names[section], order, axis=0)
        table, wanted = slot_tables(placed, first_expert, local_experts, places)
        tables.append(table)
        lane_masks.append(wanted)
        named.append(named_mask(placed))
    home = [
        lax.dynamic_index_in_dim(value, row * col_count + col, 0, keepdims=False).T for value in names
    ]
    slots = local_experts * places
    pick = (
        jnp.arange(LANES, dtype=jnp.int32)[None, :]
        == (first_expert + jnp.arange(slots, dtype=jnp.int32) // places)[:, None]
    ).astype(F32)

    offset = col * tokens
    docs = lax.dynamic_index_in_dim(doc_ids, pipe, 0, keepdims=False)
    doc_query = lax.dynamic_slice_in_dim(docs, offset, tokens, 0)
    query_place = offset + jnp.arange(tokens, dtype=jnp.int32)
    allowed = (query_place[:, None] >= jnp.arange(length, dtype=jnp.int32)[None, :]) & (
        doc_query[:, None] == docs[None, :]
    )
    mask = jnp.where(allowed, 0.0, MASKED).astype(F32)
    falling = jnp.concatenate(
        [buckets[-1:], jnp.flip(buckets), jnp.zeros((length,), jnp.int32)], axis=0
    )
    by_place = jnp.concatenate(
        [
            lax.dynamic_slice_in_dim(falling, length - offset, length, 0),
            lax.dynamic_slice_in_dim(falling, length - offset - tokens, tokens, 0),
        ],
        axis=0,
    )
    bucket_hot = jnp.arange(NBUCKET, dtype=jnp.int32)[:, None] == by_place[None, :]
    diagonals = [
        jnp.einsum(
            "bh,bx->hx", value["table"], bucket_hot.astype(BF), preferred_element_type=F32
        ).reshape(HEADS // 2, 2, -1)
        for value in params
    ]

    stream = lax.dynamic_index_in_dim(section_input, pipe, 0, keepdims=False)
    results = []
    kept = []
    for section in range(2):
        weight = params[section]
        normed_attn = norm_scale(stream, weight["gain_attn"]).astype(BF)
        sequence = gather_sequence(normed_attn)
        q = jnp.dot(normed_attn, weight["q"], preferred_element_type=F32).astype(BF)
        key = jnp.dot(sequence, weight["k"], preferred_element_type=F32).astype(BF)
        value = jnp.dot(sequence, weight["v"], preferred_element_type=F32).astype(BF)
        attended, lse = attention_forward(q, key, value, diagonals[section], mask)
        after_attn = stream + jnp.dot(attended, weight["out"], preferred_element_type=F32)
        normed_moe = norm_scale(after_attn, weight["gain_moe"]).astype(BF)
        part, rows, gates = expert_forward(
            section, pipe_word, tables[section], gather_tokens(normed_moe), named[section], pick,
            weight["router"], expert_weights,
        )
        result = after_attn + scatter_tokens(part)
        kept.append(
            (stream, normed_attn, sequence, q, key, value, lse, attended, after_attn, normed_moe, rows, gates)
        )
        results.append(result)
        stream = result

    grad = lax.dynamic_index_in_dim(cotangent, pipe, 0, keepdims=False)
    lane_ids = jnp.arange(LANES, dtype=jnp.int32)[None, :]
    input_grads = [None, None]
    dense = [None, None]
    stores = None
    for section in (1, 0):
        weight = params[section]
        (
            stream, normed_attn, sequence, q, key, value, lse, attended, after_attn, normed_moe, rows, gates
        ) = kept[section]
        part, stores = expert_backward(
            section, pipe_word, tables[section], gather_tokens(grad.astype(BF)), rows, gates,
            lane_masks[section], expert_weights, stores,
        )
        named_by = home[section]
        logits = jnp.dot(normed_moe, weight["router"], preferred_element_type=F32)
        chosen = jnp.stack(
            [
                jnp.sum(jnp.where(named_by[:, k : k + 1] == lane_ids, logits, 0.0), axis=1)
                for k in range(TOP)
            ],
            axis=1,
        )
        chosen = jnp.exp(chosen - jnp.max(chosen, axis=1, keepdims=True))
        gate_weights = chosen / jnp.sum(chosen, axis=1, keepdims=True)
        summed = scatter_tokens(part)
        grad_gate = summed[tokens, : TOP * tokens].reshape(TOP, tokens).T
        grad_chosen = gate_weights * (
            grad_gate - jnp.sum(gate_weights * grad_gate, axis=1, keepdims=True)
        )
        grad_logits = jnp.zeros((tokens, LANES), F32)
        for k in range(TOP):
            grad_logits = grad_logits + jnp.where(
                named_by[:, k : k + 1] == lane_ids, grad_chosen[:, k : k + 1], 0.0
            )
        grad_logits = grad_logits.astype(BF)
        grad_router = jnp.einsum("td,te->de", normed_moe, grad_logits, preferred_element_type=F32)
        grad_normed = summed[:tokens] + jnp.einsum(
            "te,de->td", grad_logits, weight["router"], preferred_element_type=F32
        )
        _, norm_back = jax.vjp(norm_scale, after_attn, weight["gain_moe"])
        grad_after, grad_gain_moe = norm_back(grad_normed)
        grad_after = grad + grad_after
        grad_branch = grad_after.astype(BF)
        grad_attended = jnp.einsum(
            "td,cd->tc", grad_branch, weight["out"], preferred_element_type=F32
        ).astype(BF)
        dq, dk, dv, dist = attention_backward(
            q, key, value, grad_attended, lse, diagonals[section], mask
        )
        partial = jnp.einsum("td,cd->tc", dk, weight["k"], preferred_element_type=F32) + jnp.einsum(
            "td,cd->tc", dv, weight["v"], preferred_element_type=F32
        )
        partial = partial.astype(BF)
        if section == 0:
            kept_in, kept_out, sent_in, sent_out = stores
            total_in = kept_in.astype(F32) + swap_pipe(sent_in).astype(F32)
            total_out = kept_out.astype(F32) + swap_pipe(sent_out).astype(F32)
        grad_normed = scatter_sequence(partial) + jnp.einsum(
            "td,cd->tc", dq, weight["q"], preferred_element_type=F32
        )
        _, norm_back = jax.vjp(norm_scale, stream, weight["gain_attn"])
        grad_stream, grad_gain_attn = norm_back(grad_normed)
        grad = grad_after + grad_stream
        input_grads[section] = grad
        dist = dist.reshape(HEADS, 8, -1)
        by_distance = dist[:, 0]
        for turn in range(1, 8):
            by_distance = by_distance + jnp.roll(dist[:, turn], -turn, axis=1)
        grad_table = jnp.einsum(
            "bx,hx->bh", bucket_hot.astype(F32), by_distance, precision=HIGH, preferred_element_type=F32
        )

        def lines(values):
            flat = jnp.concatenate([value.reshape(group_size, -1) for value in values], axis=1)
            flat = jnp.pad(flat, ((0, 0), (0, 2 * middle - flat.shape[1])))
            return flat.astype(BF)[:, None]

        small = jnp.concatenate(
            [
                lines([grad_router[:, :EXPERTS]]),
                lines([grad_gain_attn, grad_gain_moe, grad_table]),
                jnp.zeros((group_size, 6, 2 * middle), BF),
            ],
            axis=1,
        )
        large = dense_grads(normed_attn, sequence, attended, dq, dk, dv, grad_branch)
        packed = jnp.concatenate([large.reshape(group_size, shard, -1), small], axis=1)
        sent = lax.ppermute(packed, "pipe", [(1 - section, section)])
        dense[section] = packed.astype(F32) + sent.astype(F32)

    summed = scatter_absolute(jnp.where(first, dense[0], dense[1]).astype(BF), order)
    flat = summed[shard:]

    def by_micro_batch(values):
        own = jnp.where(first, values[0], values[1])
        other = swap_pipe(jnp.where(first, values[1], values[0]))
        return jnp.where(first, jnp.stack([own, other]), jnp.stack([other, own]))[None]

    return (
        by_micro_batch(results),
        by_micro_batch(input_grads),
        summed[None, :shard, : 3 * width],
        summed[None, :shard, 3 * width :],
        flat[0, : shard * EXPERTS].reshape(1, shard, EXPERTS),
        flat[1, :shard][None],
        flat[1, shard : 2 * shard][None],
        flat[1, 2 * shard : 2 * shard + bias_count][None],
        total_in[None],
        total_out[None],
    )


def solution(mesh):
    return jax.shard_map(
        on_device,
        mesh=mesh,
        in_specs=(
            P(None, ("row", "col"), None),
            P(None, ("row", "col"), None),
            P("pipe", ("row", "col"), None),
            P("pipe", ("row", "col"), None),
            P("pipe", ("row", "col"), None),
            P("pipe", ("row", "col")),
            P("pipe", ("row", "col")),
            P("pipe", ("row", "col")),
            P("pipe", "row", None, "col"),
            P("pipe", "row", "col", None),
            P("pipe", None, ("row", "col"), None),
            P(None, "row"),
            P(),
        ),
        out_specs=(
            P("pipe", None, ("row", "col"), None),
            P("pipe", None, ("row", "col"), None),
            P("pipe", ("row", "col"), None),
            P("pipe", ("row", "col"), None),
            P("pipe", ("row", "col"), None),
            P("pipe", ("row", "col")),
            P("pipe", ("row", "col")),
            P("pipe", ("row", "col")),
            P("pipe", "row", None, "col"),
            P("pipe", "row", "col", None),
        ),
        check_vma=False,
    )
```

time: 3440 us -> 1260 us (0.37)
  local copies, waits for them, and re-layouts: 893 us -> 98.6 us
  blocking collectives: 597 us -> 0 us
  waiting for transfers between devices: 976 us -> 403 us
  matrix products: 611 us -> 40.4 us
  Pallas kernels: 0 us -> 262 us
  starting transfers between devices: 42.8 us -> 248 us
  other arithmetic: 261 us -> 140 us
    dot_general x100 -> x30, matrix products: 611 us -> 40.4 us  [the longest x2 7.97 us: on_device(): key = jnp.dot(sequence, weight['k'], preferred_element_type=F32).astype(BF)]
    all_gather x14 -> x1, waiting for transfers between devices: 518 us -> 0.01 us  [on_device(): later = lax.all_gather(later, ('row', 'col'), axis=0)]
    rev x4 -> x1, local copies, waits for them, and re-layouts: 404 us -> 0.08 us  [on_device(): jnp.flip(buckets)]
    ppermute x4 -> x213, waiting for transfers between devices: 5.32 us -> 403 us  [the longest x42 197 us: shift_col(): lax.ppermute(value, 'col', [(i, (i + distance) % count) for i in range(co...]
    all_to_all x10 -> x0, blocking collectives: 342 us -> none  [the longest x4 228 us: expert_trip(): lax.all_to_all(partial_value.astype(jnp.bfloat16), 'row', split_axis=1, c...]
    all_to_all x8 -> x0, waiting for transfers between devices: 300 us -> none  [the longest x6 270 us: expert_trip(): lax.all_to_all(lax.all_to_all(partial_value.astype(jnp.bfloat16), 'row',...]
    pallas_call x0 -> x10, Pallas kernels: none -> 262 us  [the longest x2 96 us: expert_backward(): pl.pallas_call(functools.partial(expert_bwd_kernel, section, group, steps...]
    ppermute x4 -> x213, starting transfers between devices: 0.01 us -> 248 us  [the longest x42 71 us: shift_col(): lax.ppermute(value, 'col', [(i, (i + distance) % count) for i in range(co...]
  transfers between devices with their start and end apart: 35 -> 214, of which waited for: 23 -> 102; matrix products, arithmetic and copies ran while one was open for 39% -> 20% of each run, Pallas kernels for 0% -> 17%
where the time goes in v1:
time: 1260 us; the launch traced here: 1240 us
  waiting for transfers between devices  403 us (32%)
  Pallas kernels  262 us (21%)
  starting transfers between devices  248 us (20%)
  other arithmetic  140 us (11%)
  local copies, waits for them, and re-layouts  98.6 us (8%)
  between operations  49.8 us (4%)
  matrix products  40.4 us (3%)
    ppermute x42, waiting for transfers between devices, shift_col(): lax.ppermute(value, 'col', [(i, (i + distance) % count) for i in range(co...  197 us
    pallas_call x2, Pallas kernels, expert_backward(): pl.pallas_call(functools.partial(expert_bwd_kernel, section, group, steps...  96 us
    pallas_call x2, Pallas kernels, expert_forward(): pl.pallas_call(functools.partial(expert_fwd_kernel, section, group, steps...  76 us
    ppermute x42, starting transfers between devices, shift_col(): lax.ppermute(value, 'col', [(i, (i + distance) % count) for i in range(co...  71 us
    ppermute x20, waiting for transfers between devices, scatter_groups(): from_y = lax.ppermute(for_y, 'row', Y_PAIRS)  43.7 us
    ppermute x20, waiting for transfers between devices, scatter_groups(): left = lax.ppermute(left, 'row', X_PAIRS)  39.5 us
    pallas_call x2, Pallas kernels, attention_backward(): pl.pallas_call(attention_bwd_kernel, grid=(pairs,), in_specs=[pl.BlockSpe...  39.4 us
    broadcast_in_dim x1, other arithmetic, on_device(): total_in[None]  32 us
  transfers between devices with their start and end apart: 214, of which 102 were waited for; matrix products, arithmetic and copies ran while one was open for 20% of the time, Pallas kernels for 17%

profile of v1, /device:TPU:0, one launch (start us, length us, event | category | flops | bytes accessed | tf_op | source)
XLA Modules:
  0.0 1241.0 jit_solution(17214973060068561109)
XLA Ops:
  136.3 13.9 %collective-permute-done.22 = bf16[256,768]{1,0:T(8,128)(2,1)S(1)} collective-permute-done((bf16[256,768]{1,0:T(8,128)(2,1)}, bf16[256,768]{1,0:T(8,128)(2,1)S(1)}, u32[]{:S(2)}, u32[]{:S(2)}) %collective-permute-start.22) | collective-permute-done | bytes 393248 | tf_op jit(solution)/shard_map/ppermute | solution.py:43
  154.0 17.8 %collective-permute-done.23 = bf16[256,768]{1,0:T(8,128)(2,1)S(1)} collective-permute-done((bf16[256,768]{1,0:T(8,128)(2,1)S(1)}, bf16[256,768]{1,0:T(8,128)(2,1)S(1)}, u32[]{:S(2)}, u32[]{:S(2)}) %collective-permute-start.23) | collective-permute-done | bytes 393248 | tf_op jit(solution)/shard_map/ppermute | solution.py:43
  180.5 13.3 %attention_forward.2 = (bf16[256,768]{1,0:T(8,128)(2,1)}, f32[256,768]{1,0:T(8,128)}) custom-call(bf16[256,768]{1,0:T(8,128)(2,1)} %convolution_convert_fusion.7.q_ref, bf16[1024,768]{1,0:T(8,128)(2,1)} %convolution_convert_fusion.3.k_ref, bf16[1024,768]{1,0:T(8,128)(2,1)} %convolution_convert_fusion.2.v_ref, f32[6,2,1280]{2,1,0:T(2,128)} %copy.77.diag_ref, ...), custom_call_target="tpu_custom_call" | custom-call | flops 805306368 | bytes 6291456 | tf_op jit(solution)/shard_map/attention_forward/pallas_call | solution.py:198
  197.8 8.0 collective-permute-done.25.refs_3_
  212.6 8.1 collective-permute-done.27.refs_5_
  222.7 7.1 collective-permute-done.29.refs_7_
  233.4 8.7 collective-permute-done.34.refs_12_
  243.5 7.0 collective-permute-done.39.refs_17_
  262.7 38.0 %expert_forward.2 = (bf16[256,768]{1,0:T(8,128)(2,1)}, bf16[256,768]{1,0:T(8,128)(2,1)}, bf16[256,768]{1,0:T(8,128)(2,1)}, bf16[256,384]{1,0:T(8,128)(2,1)}, bf1...) custom-call(s32[1]{0:T(128)} %bitcast.46.refs_0_, ...), custom_call_target="tpu_custom_call" | custom-call | flops 9663676416 | bytes 62914560 | tf_op jit(solution)/shard_map/expert_forward/pallas_call | solution.py:577
  312.1 7.1 collective-permute-done.52
  322.0 5.0 collective-permute-done.57
  363.8 4.7 collective-permute-start.49
  372.5 25.1 %collective-permute-done.54 = bf16[256,768]{1,0:T(8,128)(2,1)S(1)} collective-permute-done((bf16[256,768]{1,0:T(8,128)(2,1)S(1)}, bf16[256,768]{1,0:T(8,128)(2,1)S(1)}, u32[]{:S(2)}, u32[]{:S(2)}) %collective-permute-start.54) | collective-permute-done | bytes 393248 | tf_op jit(solution)/shard_map/ppermute | solution.py:43
  402.6 7.8 collective-permute-done.121.refs_16_
  431.3 10.2 collective-permute-done.66
  446.3 4.8 collective-permute-done.67
  459.8 13.2 %attention_forward.3 = (bf16[256,768]{1,0:T(8,128)(2,1)}, f32[256,768]{1,0:T(8,128)}) custom-call(bf16[256,768]{1,0:T(8,128)(2,1)} %convolution_convert_fusion.6.q_ref, bf16[1024,768]{1,0:T(8,128)(2,1)} %convolution_convert_fusion.1.k_ref, bf16[1024,768]{1,0:T(8,128)(2,1)} %convolution_convert_fusion.v_ref, f32[6,2,1280]{2,1,0:T(2,128)} %copy.81.diag_ref, ...), custom_call_target="tpu_custom_call" | custom-call | flops 805306368 | bytes 6291456 | tf_op jit(solution)/shard_map/attention_forward/pallas_call | solution.py:198
  476.1 9.9 collective-permute-done.72.refs_6_
  545.2 38.0 %expert_forward.3 = (bf16[256,768]{1,0:T(8,128)(2,1)}, bf16[256,768]{1,0:T(8,128)(2,1)}, bf16[256,768]{1,0:T(8,128)(2,1)}, bf16[256,384]{1,0:T(8,128)(2,1)}, bf1...) custom-call(s32[1]{0:T(128)} %bitcast.46.refs_0_, ...), custom_call_target="tpu_custom_call" | custom-call | flops 9663676416 | bytes 62914560 | tf_op jit(solution)/shard_map/expert_forward/pallas_call | solution.py:577
  594.5 48.0 %expert_backward.2 = (bf16[272,768]{1,0:T(8,128)(2,1)}, bf16[272,768]{1,0:T(8,128)(2,1)}, bf16[272,768]{1,0:T(8,128)(2,1)}, bf16[272,384]{1,0:T(8,128)(2,1)}, bf...) custom-call(s32[1]{0:T(128)} %bitcast.46.refs_0_, ...), custom_call_target="tpu_custom_call" | custom-call | flops 24159191040 | bytes 100663296 | tf_op jit(solution)/shard_map/expert_backward/pallas_call | solution.py:773
  663.8 6.0 collective-permute-done.133
  680.5 5.8 collective-permute-done.100
  689.6 5.7 collective-permute-done.139
  697.8 4.9 collective-permute-done.134
  732.1 12.2 collective-permute-done.135
  744.3 24.1 %collective-permute-start.91 = (bf16[256,768]{1,0:T(8,128)(2,1)}, bf16[256,768]{1,0:T(8,128)(2,1)}, u32[]{:S(2)}, u32[]{:S(2)}) collective-permute-start(bf16[256,768]{1,0:T(8,128)(2,1)} %add_convert_fusion.10), channel_id=1, source_target_pairs={{0,1},{1,2},{2,3},{3,0},{4,5},{5,6},{6,7},{7,4},{8,9},{9,10},{10,1... | collective-permute-start | bytes 1179656 | tf_op jit(solution)/shard_map/ppermute | solution.py:43
  772.9 19.7 %attention_backward.2 = (bf16[256,768]{1,0:T(8,128)(2,1)}, bf16[1024,768]{1,0:T(8,128)(2,1)}, bf16[1024,768]{1,0:T(8,128)(2,1)}, f32[6,2,8,1280]{3,2,1,0:T(8,128)}) custom-call(bf16[256,768]{1,0:T(8,128)(2,1)} %convolution_convert_fusion.6.q_ref, bf16[1024,768]{1,0:T(8,128)(2,1)} %convolution_convert_fusion.1.k_ref, ...), custom_call_target="tpu_custom_call" | custom-call | flops 2013265920 | bytes 9437184 | tf_op jit(solution)/shard_map/attention_backward/pallas_call | solution.py:270
  802.0 4.9 collective-permute-done.145
  806.9 8.2 collective-permute-done.147
  815.1 8.9 collective-permute-done.146
  828.8 9.6 collective-permute-done.152.refs_6_
  871.6 11.7 dense_grads.3
  884.3 48.0 %expert_backward.3 = (bf16[272,768]{1,0:T(8,128)(2,1)}, bf16[272,768]{1,0:T(8,128)(2,1)}, bf16[272,768]{1,0:T(8,128)(2,1)}, bf16[272,384]{1,0:T(8,128)(2,1)}, bf...) custom-call(s32[1]{0:T(128)} %bitcast.46.refs_0_, ...), custom_call_target="tpu_custom_call", output_to_operand_aliasing={{20}: (29, {}), {21}: (30, {}), {22}: (31, {}), {23}: (32, ... | custom-call | flops 24159191040 | bytes 100663296 | tf_op jit(solution)/shard_map/expert_backward/pallas_call | solution.py:773
  943.1 6.0 collective-permute-done.179
  950.0 5.0 collective-permute-done.184
  963.6 6.1 collective-permute-done.180
  983.6 12.9 %collective-permute-done.176 = bf16[272,768]{1,0:T(8,128)(2,1)} collective-permute-done((bf16[272,768]{1,0:T(8,128)(2,1)}, bf16[272,768]{1,0:T(8,128)(2,1)}, u32[]{:S(2)}, u32[]{:S(2)}) %collective-permute-start.176) | collective-permute-done | bytes 417824 | tf_op jit(solution)/shard_map/ppermute | solution.py:43
  1002.4 19.7 %attention_backward.3 = (bf16[256,768]{1,0:T(8,128)(2,1)}, bf16[1024,768]{1,0:T(8,128)(2,1)}, bf16[1024,768]{1,0:T(8,128)(2,1)}, f32[6,2,8,1280]{3,2,1,0:T(8,128)}) custom-call(bf16[256,768]{1,0:T(8,128)(2,1)} %convolution_convert_fusion.7.q_ref, bf16[1024,768]{1,0:T(8,128)(2,1)} %convolution_convert_fusion.3.k_ref, ...), custom_call_target="tpu_custom_call" | custom-call | flops 2013265920 | bytes 9437184 | tf_op jit(solution)/shard_map/attention_backward/pallas_call | solution.py:270
  1037.2 11.9 dense_grads.2
  1049.2 7.5 collective-permute-done.187
  1060.0 8.2 maximum_maximum_fusion
  1079.2 5.8 collective-permute-done.191
  1085.0 5.2 select_convert_fusion
  1115.1 5.6 collective-permute-done.192
  1123.9 6.6 collective-permute-done.195
  1166.2 10.8 collective-permute-done.201
  1180.6 32.0 %add_bitcast_fusion.1 = f32[1,16,768,768]{3,2,1,0:T(8,128)} fusion(bf16[16,768,768]{2,1,0:T(8,128)(2,1)} %collective-permute-done.211, bf16[16,768,768]{2,1,0:T(8,128)(2,1)} %get-tuple-element.221), kind=kLoop, calls=%fused_computation.5 | loop fusion | flops 28311552 | bytes 75497472 | tf_op jit(solution)/shard_map/broadcast_in_dim | solution.py:1150
  1212.6 21.0 %add_bitcast_fusion = f32[1,16,768,768]{3,2,1,0:T(8,128)} fusion(bf16[16,768,768]{2,1,0:T(8,128)(2,1)} %collective-permute-done.212, bf16[16,768,768]{2,1,0:T(8,128)(2,1)S(1)} %bitcast.318), kind=kLoop, calls=%fused_computation.4 | loop fusion | flops 28311552 | bytes 75497472 | tf_op jit(solution)/shard_map/broadcast_in_dim | solution.py:1151
  (1290 shorter events, 561.4 us)
Async XLA Ops:
  7.2 331.7 %all-gather.3.cloned.1.call-start = ((), (), s32[]{:S(2)}) async-start(), calls=%async_computation | async-start | bytes 2506752 | tf_op jit(solution)/shard_map/all_gather | solution.py:941
  10.6 251.4 %collective-permute-start.43 = (bf16[16,768,768]{2,1,0:T(8,128)(2,1)}, bf16[16,768,768]{2,1,0:T(8,128)(2,1)}, u32[]{:S(2)}, u32[]{:S(2)}) collective-permute-start(bf16[16,768,768]{2,1,0:T(8,128)(2,1)} %bitcast.307), channel_id=1, source_target_pairs={{0,16},{16,0},{1,17},{17,1},{2,18},{18,2},{3,19},{19,3},{4,20},{20... | collective-permute-start | bytes 56623112 | tf_op jit(solution)/shard_map/ppermute | solution.py:38
  11.0 251.0 %collective-permute-start.44 = (bf16[16,768,768]{2,1,0:T(8,128)(2,1)}, bf16[16,768,768]{2,1,0:T(8,128)(2,1)}, u32[]{:S(2)}, u32[]{:S(2)}) collective-permute-start(bf16[16,768,768]{2,1,0:T(8,128)(2,1)} %bitcast.312), channel_id=1, source_target_pairs={{0,16},{16,0},{1,17},{17,1},{2,18},{18,2},{3,19},{19,3},{4,20},{20... | collective-permute-start | bytes 56623112 | tf_op jit(solution)/shard_map/ppermute | solution.py:38
  114.2 19.1 %collective-permute-start.21 = (bf16[256,768]{1,0:T(8,128)(2,1)S(1)}, bf16[256,768]{1,0:T(8,128)(2,1)}, u32[]{:S(2)}, u32[]{:S(2)}) collective-permute-start(bf16[256,768]{1,0:T(8,128)(2,1)S(1)} %get-tuple-element.262.normed_ref), channel_id=1, source_target_pairs={{0,1},{1,2},{2,3},{3,0},{4,5},{5,6},{6,7},{7,4},{8,9},{9,10},{10,1... | collective-permute-start | bytes 1179656 | tf_op jit(solution)/shard_map/ppermute | solution.py:43
  150.2 21.6 %collective-permute-start.23 = (bf16[256,768]{1,0:T(8,128)(2,1)S(1)}, bf16[256,768]{1,0:T(8,128)(2,1)S(1)}, u32[]{:S(2)}, u32[]{:S(2)}) collective-permute-start(bf16[256,768]{1,0:T(8,128)(2,1)S(1)} %collective-permute-done.22), channel_id=1, source_target_pairs={{0,1},{1,2},{2,3},{3,0},{4,5},{5,6},{6,7},{7,4},{8,9},{9,10},{10,1... | collective-permute-start | bytes 1179656 | tf_op jit(solution)/shard_map/ppermute | solution.py:43
  303.7 32.8 %collective-permute-start.111 = (bf16[256,768]{1,0:T(8,128)(2,1)S(1)}, bf16[256,768]{1,0:T(8,128)(2,1)}, u32[]{:S(2)}, u32[]{:S(2)}) collective-permute-start(bf16[256,768]{1,0:T(8,128)(2,1)S(1)} %bitcast_convert_fusion.refs_1_), channel_id=1, source_target_pairs={{0,1},{1,2},{2,3},{3,0},{4,5},{5,6},{6,7},{7,4},{8,9},{9,10},{10,1... | collective-permute-start | bytes 1179656 | tf_op jit(solution)/shard_map/ppermute | solution.py:43
  307.9 22.6 %collective-permute-start.45 = (bf16[256,384]{1,0:T(8,128)(2,1)S(1)}, bf16[256,384]{1,0:T(8,128)(2,1)S(1)}, u32[]{:S(2)}, u32[]{:S(2)}) collective-permute-start(bf16[256,384]{1,0:T(8,128)(2,1)S(1)} %copy-done.210), channel_id=1, source_target_pairs={{0,8},{4,12},{8,0},{12,4},{1,9},{5,13},{9,1},{13,5},{2,10},{6,14},... | collective-permute-start | bytes 589832 | tf_op jit(solution)/shard_map/ppermute | solution.py:83
  309.1 22.2 %collective-permute-start.47 = (bf16[256,384]{1,0:T(8,128)(2,1)S(1)}, bf16[256,384]{1,0:T(8,128)(2,1)S(1)}, u32[]{:S(2)}, u32[]{:S(2)}) collective-permute-start(bf16[256,384]{1,0:T(8,128)(2,1)S(1)} %copy-done.209), channel_id=1, source_target_pairs={{0,4},{4,0},{8,12},{12,8},{1,5},{5,1},{9,13},{13,9},{2,6},{6,2},{1... | collective-permute-start | bytes 589832 | tf_op jit(solution)/shard_map/ppermute | solution.py:82
  338.9 89.7 %collective-permute-start.64 = (bf16[16,48,1536]{2,1,0:T(8,128)(2,1)}, bf16[16,48,1536]{2,1,0:T(8,128)(2,1)}, u32[]{:S(2)}, u32[]{:S(2)}) collective-permute-start(bf16[16,48,1536]{2,1,0:T(8,128)(2,1)} %bitcast.343), channel_id=1, source_target_pairs={{0,16},{16,0},{1,17},{17,1},{2,18},{18,2},{3,19},{19,3},{4,20},{20... | collective-permute-start | bytes 7077896 | tf_op jit(solution)/shard_map/ppermute | solution.py:38
  362.1 35.4 %collective-permute-start.54 = (bf16[256,768]{1,0:T(8,128)(2,1)S(1)}, bf16[256,768]{1,0:T(8,128)(2,1)S(1)}, u32[]{:S(2)}, u32[]{:S(2)}) collective-permute-start(bf16[256,768]{1,0:T(8,128)(2,1)S(1)} %add_convert_fusion.12), channel_id=1, source_target_pairs={{0,2},{1,3},{2,0},{3,1},{4,6},{5,7},{6,4},{7,5},{8,10},{9,11},{10,... | collective-permute-start | bytes 1179656 | tf_op jit(solution)/shard_map/ppermute | solution.py:43
  363.8 34.5 %collective-permute-start.49 = (bf16[256,768]{1,0:T(8,128)(2,1)S(1)}, bf16[256,768]{1,0:T(8,128)(2,1)}, u32[]{:S(2)}, u32[]{:S(2)}) collective-permute-start(bf16[256,768]{1,0:T(8,128)(2,1)S(1)} %add_convert_fusion.13), channel_id=1, source_target_pairs={{0,1},{1,2},{2,3},{3,0},{4,5},{5,6},{6,7},{7,4},{8,9},{9,10},{10,1... | collective-permute-start | bytes 1179656 | tf_op jit(solution)/shard_map/ppermute | solution.py:43
  368.5 31.9 %collective-permute-start.107 = (bf16[256,768]{1,0:T(8,128)(2,1)S(1)}, bf16[256,768]{1,0:T(8,128)(2,1)}, u32[]{:S(2)}, u32[]{:S(2)}) collective-permute-start(bf16[256,768]{1,0:T(8,128)(2,1)S(1)} %bitcast_convert_fusion.refs_1_), channel_id=1, source_target_pairs={{0,4},{4,0},{8,12},{12,8},{1,5},{5,1},{9,13},{13,9},{2,6},{6,2},{1... | collective-permute-start | bytes 1179656 | tf_op jit(solution)/shard_map/ppermute | solution.py:67
  371.7 30.8 %collective-permute-start.113 = (bf16[256,768]{1,0:T(8,128)(2,1)}, bf16[256,768]{1,0:T(8,128)(2,1)}, u32[]{:S(2)}, u32[]{:S(2)}) collective-permute-start(bf16[256,768]{1,0:T(8,128)(2,1)} %collective-permute-done.111.refs_6_), channel_id=1, source_target_pairs={{0,8},{4,12},{8,0},{12,4},{1,9},{5,13},{9,1},{13,5},{2,10},{6,14},... | collective-permute-start | bytes 1179656 | tf_op jit(solution)/shard_map/ppermute | solution.py:68
  421.2 75.6 %collective-permute-start.109 = (bf16[256,384]{1,0:T(8,128)(2,1)}, bf16[256,384]{1,0:T(8,128)(2,1)}, u32[]{:S(2)}, u32[]{:S(2)}) collective-permute-start(bf16[256,384]{1,0:T(8,128)(2,1)} %slice.1053), channel_id=1, source_target_pairs={{0,4},{4,0},{8,12},{12,8},{1,5},{5,1},{9,13},{13,9},{2,6},{6,2},{1... | collective-permute-start | bytes 589832 | tf_op jit(solution)/shard_map/ppermute | solution.py:69
  496.8 19.3 %collective-permute-start.73 = (bf16[256,768]{1,0:T(8,128)(2,1)}, bf16[256,768]{1,0:T(8,128)(2,1)}, u32[]{:S(2)}, u32[]{:S(2)}) collective-permute-start(bf16[256,768]{1,0:T(8,128)(2,1)} %collective-permute-done.72.refs_6_), channel_id=1, source_target_pairs={{0,4},{4,0},{8,12},{12,8},{1,5},{5,1},{9,13},{13,9},{2,6},{6,2},{1... | collective-permute-start | bytes 1179656 | tf_op jit(solution)/shard_map/ppermute | solution.py:67
  539.5 49.8 %collective-permute-start.115 = (bf16[256,384]{1,0:T(8,128)(2,1)S(1)}, bf16[256,384]{1,0:T(8,128)(2,1)S(1)}, u32[]{:S(2)}, u32[]{:S(2)}) collective-permute-start(bf16[256,384]{1,0:T(8,128)(2,1)S(1)} %copy-done.131), channel_id=1, source_target_pairs={{0,8},{4,12},{8,0},{12,4},{1,9},{5,13},{9,1},{13,5},{2,10},{6,14},... | collective-permute-start | bytes 589832 | tf_op jit(solution)/shard_map/ppermute | solution.py:70
  540.9 49.4 %collective-permute-start.119 = (bf16[256,384]{1,0:T(8,128)(2,1)S(1)}, bf16[256,384]{1,0:T(8,128)(2,1)S(1)}, u32[]{:S(2)}, u32[]{:S(2)}) collective-permute-start(bf16[256,384]{1,0:T(8,128)(2,1)S(1)} %copy-done.129), channel_id=1, source_target_pairs={{0,4},{4,0},{8,12},{12,8},{1,5},{5,1},{9,13},{13,9},{2,6},{6,2},{1... | collective-permute-start | bytes 589832 | tf_op jit(solution)/shard_map/ppermute | solution.py:69
  541.4 50.0 %collective-permute-start.120 = (bf16[256,384]{1,0:T(8,128)(2,1)S(1)}, bf16[256,384]{1,0:T(8,128)(2,1)S(1)}, u32[]{:S(2)}, u32[]{:S(2)}) collective-permute-start(bf16[256,384]{1,0:T(8,128)(2,1)S(1)} %copy-done.130), channel_id=1, source_target_pairs={{0,8},{4,12},{8,0},{12,4},{1,9},{5,13},{9,1},{13,5},{2,10},{6,14},... | collective-permute-start | bytes 589832 | tf_op jit(solution)/shard_map/ppermute | solution.py:70
  543.1 49.2 %collective-permute-start.124 = (bf16[256,384]{1,0:T(8,128)(2,1)S(1)}, bf16[256,384]{1,0:T(8,128)(2,1)S(1)}, u32[]{:S(2)}, u32[]{:S(2)}) collective-permute-start(bf16[256,384]{1,0:T(8,128)(2,1)S(1)} %copy-done.128), channel_id=1, source_target_pairs={{0,4},{4,0},{8,12},{12,8},{1,5},{5,1},{9,13},{13,9},{2,6},{6,2},{1... | collective-permute-start | bytes 589832 | tf_op jit(solution)/shard_map/ppermute | solution.py:69
  544.1 49.3 %collective-permute-start.125 = (bf16[256,384]{1,0:T(8,128)(2,1)S(1)}, bf16[256,384]{1,0:T(8,128)(2,1)S(1)}, u32[]{:S(2)}, u32[]{:S(2)}) collective-permute-start(bf16[256,384]{1,0:T(8,128)(2,1)S(1)} %copy-done.127), channel_id=1, source_target_pairs={{0,8},{4,12},{8,0},{12,4},{1,9},{5,13},{9,1},{13,5},{2,10},{6,14},... | collective-permute-start | bytes 589832 | tf_op jit(solution)/shard_map/ppermute | solution.py:70
  589.2 59.4 %collective-permute-start.87 = (bf16[256,384]{1,0:T(8,128)(2,1)S(1)}, bf16[256,384]{1,0:T(8,128)(2,1)S(1)}, u32[]{:S(2)}, u32[]{:S(2)}) collective-permute-start(bf16[256,384]{1,0:T(8,128)(2,1)S(1)} %copy-done.207), channel_id=1, source_target_pairs={{0,8},{4,12},{8,0},{12,4},{1,9},{5,13},{9,1},{13,5},{2,10},{6,14},... | collective-permute-start | bytes 589832 | tf_op jit(solution)/shard_map/ppermute | solution.py:83
  590.3 59.6 %collective-permute-start.89 = (bf16[256,384]{1,0:T(8,128)(2,1)S(1)}, bf16[256,384]{1,0:T(8,128)(2,1)S(1)}, u32[]{:S(2)}, u32[]{:S(2)}) collective-permute-start(bf16[256,384]{1,0:T(8,128)(2,1)S(1)} %copy-done.205), channel_id=1, source_target_pairs={{0,4},{4,0},{8,12},{12,8},{1,5},{5,1},{9,13},{13,9},{2,6},{6,2},{1... | collective-permute-start | bytes 589832 | tf_op jit(solution)/shard_map/ppermute | solution.py:82
  591.5 59.6 %collective-permute-start.92 = (bf16[256,384]{1,0:T(8,128)(2,1)}, bf16[256,384]{1,0:T(8,128)(2,1)S(1)}, u32[]{:S(2)}, u32[]{:S(2)}) collective-permute-start(bf16[256,384]{1,0:T(8,128)(2,1)} %get-tuple-element.150), channel_id=1, source_target_pairs={{0,8},{4,12},{8,0},{12,4},{1,9},{5,13},{9,1},{13,5},{2,10},{6,14},... | collective-permute-start | bytes 589832 | tf_op jit(solution)/shard_map/ppermute | solution.py:83
  592.4 59.9 %collective-permute-start.94 = (bf16[256,384]{1,0:T(8,128)(2,1)}, bf16[256,384]{1,0:T(8,128)(2,1)S(1)}, u32[]{:S(2)}, u32[]{:S(2)}) collective-permute-start(bf16[256,384]{1,0:T(8,128)(2,1)} %get-tuple-element.152), channel_id=1, source_target_pairs={{0,4},{4,0},{8,12},{12,8},{1,5},{5,1},{9,13},{13,9},{2,6},{6,2},{1... | collective-permute-start | bytes 589832 | tf_op jit(solution)/shard_map/ppermute | solution.py:82
  593.4 60.1 %collective-permute-start.97 = (bf16[256,384]{1,0:T(8,128)(2,1)}, bf16[256,384]{1,0:T(8,128)(2,1)S(1)}, u32[]{:S(2)}, u32[]{:S(2)}) collective-permute-start(bf16[256,384]{1,0:T(8,128)(2,1)} %get-tuple-element.155), channel_id=1, source_target_pairs={{0,8},{4,12},{8,0},{12,4},{1,9},{5,13},{9,1},{13,5},{2,10},{6,14},... | collective-permute-start | bytes 589832 | tf_op jit(solution)/shard_map/ppermute | solution.py:83
  653.5 21.9 %collective-permute-start.128 = (bf16[272,384]{1,0:T(8,128)(2,1)S(1)}, bf16[272,384]{1,0:T(8,128)(2,1)S(1)}, u32[]{:S(2)}, u32[]{:S(2)}) collective-permute-start(bf16[272,384]{1,0:T(8,128)(2,1)S(1)} %copy-done.190), channel_id=1, source_target_pairs={{0,4},{4,0},{8,12},{12,8},{1,5},{5,1},{9,13},{13,9},{2,6},{6,2},{1... | collective-permute-start | bytes 626696 | tf_op jit(solution)/shard_map/ppermute | solution.py:82
  656.6 19.9 %collective-permute-start.131 = (bf16[272,384]{1,0:T(8,128)(2,1)S(1)}, bf16[272,384]{1,0:T(8,128)(2,1)S(1)}, u32[]{:S(2)}, u32[]{:S(2)}) collective-permute-start(bf16[272,384]{1,0:T(8,128)(2,1)S(1)} %copy-done.189), channel_id=1, source_target_pairs={{0,8},{4,12},{8,0},{12,4},{1,9},{5,13},{9,1},{13,5},{2,10},{6,14},... | collective-permute-start | bytes 626696 | tf_op jit(solution)/shard_map/ppermute | solution.py:83
  677.8 18.9 %collective-permute-start.137 = (bf16[272,768]{1,0:T(8,128)(2,1)S(1)}, bf16[272,768]{1,0:T(8,128)(2,1)S(1)}, u32[]{:S(2)}, u32[]{:S(2)}) collective-permute-start(bf16[272,768]{1,0:T(8,128)(2,1)S(1)} %pad_maximum_fusion.4), channel_id=1, source_target_pairs={{0,4},{4,0},{8,12},{12,8},{1,5},{5,1},{9,13},{13,9},{2,6},{6,2},{1... | collective-permute-start | bytes 1253384 | tf_op jit(solution)/shard_map/ppermute | solution.py:90
  679.4 23.4 %collective-permute-start.134 = (bf16[272,768]{1,0:T(8,128)(2,1)S(1)}, bf16[272,768]{1,0:T(8,128)(2,1)S(1)}, u32[]{:S(2)}, u32[]{:S(2)}) collective-permute-start(bf16[272,768]{1,0:T(8,128)(2,1)S(1)} %pad_maximum_fusion.3), channel_id=1, source_target_pairs={{0,8},{4,12},{8,0},{12,4},{1,9},{5,13},{9,1},{13,5},{2,10},{6,14},... | collective-permute-start | bytes 1253384 | tf_op jit(solution)/shard_map/ppermute | solution.py:91
  686.3 19.4 %collective-permute-start.132 = (bf16[272,768]{1,0:T(8,128)(2,1)S(1)}, bf16[272,768]{1,0:T(8,128)(2,1)S(1)}, u32[]{:S(2)}, u32[]{:S(2)}) collective-permute-start(bf16[272,768]{1,0:T(8,128)(2,1)S(1)} %pad_maximum_fusion.2), channel_id=1, source_target_pairs={{0,4},{4,0},{8,12},{12,8},{1,5},{5,1},{9,13},{13,9},{2,6},{6,2},{1... | collective-permute-start | bytes 1253384 | tf_op jit(solution)/shard_map/ppermute | solution.py:90
  687.8 22.4 %collective-permute-start.129 = (bf16[272,768]{1,0:T(8,128)(2,1)S(1)}, bf16[272,768]{1,0:T(8,128)(2,1)S(1)}, u32[]{:S(2)}, u32[]{:S(2)}) collective-permute-start(bf16[272,768]{1,0:T(8,128)(2,1)S(1)} %pad_maximum_fusion.1), channel_id=1, source_target_pairs={{0,8},{4,12},{8,0},{12,4},{1,9},{5,13},{9,1},{13,5},{2,10},{6,14},... | collective-permute-start | bytes 1253384 | tf_op jit(solution)/shard_map/ppermute | solution.py:91
  695.2 20.4 %collective-permute-start.95 = (bf16[256,768]{1,0:T(8,128)(2,1)S(1)}, bf16[256,768]{1,0:T(8,128)(2,1)S(1)}, u32[]{:S(2)}, u32[]{:S(2)}) collective-permute-start(bf16[256,768]{1,0:T(8,128)(2,1)S(1)} %pad_maximum_fusion.27), channel_id=1, source_target_pairs={{0,8},{4,12},{8,0},{12,4},{1,9},{5,13},{9,1},{13,5},{2,10},{6,14},... | collective-permute-start | bytes 1179656 | tf_op jit(solution)/shard_map/ppermute | solution.py:91
  722.1 22.2 %collective-permute-start.135 = (bf16[272,768]{1,0:T(8,128)(2,1)S(1)}, bf16[272,768]{1,0:T(8,128)(2,1)S(1)}, u32[]{:S(2)}, u32[]{:S(2)}) collective-permute-start(bf16[272,768]{1,0:T(8,128)(2,1)S(1)} %add_convert_fusion.6), channel_id=1, source_target_pairs={{0,2},{1,3},{2,0},{3,1},{4,6},{5,7},{6,4},{7,5},{8,10},{9,11},{10,... | collective-permute-start | bytes 1253384 | tf_op jit(solution)/shard_map/ppermute | solution.py:43
  723.1 21.1 %collective-permute-start.130 = (bf16[272,768]{1,0:T(8,128)(2,1)S(1)}, bf16[272,768]{1,0:T(8,128)(2,1)S(1)}, u32[]{:S(2)}, u32[]{:S(2)}) collective-permute-start(bf16[272,768]{1,0:T(8,128)(2,1)S(1)} %add_convert_fusion.7), channel_id=1, source_target_pairs={{0,1},{1,2},{2,3},{3,0},{4,5},{5,6},{6,7},{7,4},{8,9},{9,10},{10,1... | collective-permute-start | bytes 1253384 | tf_op jit(solution)/shard_map/ppermute | solution.py:43
  725.4 71.7 %collective-permute-start.105 = (bf16[256,768]{1,0:T(8,128)(2,1)}, bf16[256,768]{1,0:T(8,128)(2,1)}, u32[]{:S(2)}, u32[]{:S(2)}) collective-permute-start(bf16[256,768]{1,0:T(8,128)(2,1)} %pad_maximum_fusion.31), channel_id=1, source_target_pairs={{0,8},{4,12},{8,0},{12,4},{1,9},{5,13},{9,1},{13,5},{2,10},{6,14},... | collective-permute-start | bytes 1179656 | tf_op jit(solution)/shard_map/ppermute | solution.py:91
  727.6 69.8 %collective-permute-start.103 = (bf16[256,768]{1,0:T(8,128)(2,1)S(1)}, bf16[256,768]{1,0:T(8,128)(2,1)}, u32[]{:S(2)}, u32[]{:S(2)}) collective-permute-start(bf16[256,768]{1,0:T(8,128)(2,1)S(1)} %pad_maximum_fusion.30), channel_id=1, source_target_pairs={{0,4},{4,0},{8,12},{12,8},{1,5},{5,1},{9,13},{13,9},{2,6},{6,2},{1... | collective-permute-start | bytes 1179656 | tf_op jit(solution)/shard_map/ppermute | solution.py:90
  730.0 69.9 %collective-permute-start.101 = (bf16[256,768]{1,0:T(8,128)(2,1)}, bf16[256,768]{1,0:T(8,128)(2,1)}, u32[]{:S(2)}, u32[]{:S(2)}) collective-permute-start(bf16[256,768]{1,0:T(8,128)(2,1)} %add_convert_fusion.8), channel_id=1, source_target_pairs={{0,3},{1,0},{2,1},{3,2},{4,7},{5,4},{6,5},{7,6},{8,11},{9,8},{10,9... | collective-permute-start | bytes 1179656 | tf_op jit(solution)/shard_map/ppermute | solution.py:43
  744.2 57.7 %collective-permute-start.96 = (bf16[256,768]{1,0:T(8,128)(2,1)}, bf16[256,768]{1,0:T(8,128)(2,1)}, u32[]{:S(2)}, u32[]{:S(2)}) collective-permute-start(bf16[256,768]{1,0:T(8,128)(2,1)} %add_convert_fusion.9), channel_id=1, source_target_pairs={{0,2},{1,3},{2,0},{3,1},{4,6},{5,7},{6,4},{7,5},{8,10},{9,11},{10,... | collective-permute-start | bytes 1179656 | tf_op jit(solution)/shard_map/ppermute | solution.py:43
  744.3 57.7 %collective-permute-start.91 = (bf16[256,768]{1,0:T(8,128)(2,1)}, bf16[256,768]{1,0:T(8,128)(2,1)}, u32[]{:S(2)}, u32[]{:S(2)}) collective-permute-start(bf16[256,768]{1,0:T(8,128)(2,1)} %add_convert_fusion.10), channel_id=1, source_target_pairs={{0,1},{1,2},{2,3},{3,0},{4,5},{5,6},{6,7},{7,4},{8,9},{9,10},{10,1... | collective-permute-start | bytes 1179656 | tf_op jit(solution)/shard_map/ppermute | solution.py:43
  800.0 24.0 %collective-permute-start.146 = (bf16[256,768]{1,0:T(8,128)(2,1)S(1)}, bf16[256,768]{1,0:T(8,128)(2,1)S(1)}, u32[]{:S(2)}, u32[]{:S(2)}) collective-permute-start(bf16[256,768]{1,0:T(8,128)(2,1)S(1)} %get-tuple-element.289), channel_id=1, source_target_pairs={{0,2},{1,3},{2,0},{3,1},{4,6},{5,7},{6,4},{7,5},{8,10},{9,11},{10,... | collective-permute-start | bytes 1179656 | tf_op jit(solution)/shard_map/ppermute | solution.py:43
  937.6 21.5 %collective-permute-start.167 = (bf16[272,384]{1,0:T(8,128)(2,1)S(1)}, bf16[272,384]{1,0:T(8,128)(2,1)S(1)}, u32[]{:S(2)}, u32[]{:S(2)}) collective-permute-start(bf16[272,384]{1,0:T(8,128)(2,1)S(1)} %copy-done.197), channel_id=1, source_target_pairs={{0,8},{4,12},{8,0},{12,4},{1,9},{5,13},{9,1},{13,5},{2,10},{6,14},... | collective-permute-start | bytes 626696 | tf_op jit(solution)/shard_map/ppermute | solution.py:83
  938.9 21.6 %collective-permute-start.169 = (bf16[272,384]{1,0:T(8,128)(2,1)S(1)}, bf16[272,384]{1,0:T(8,128)(2,1)S(1)}, u32[]{:S(2)}, u32[]{:S(2)}) collective-permute-start(bf16[272,384]{1,0:T(8,128)(2,1)S(1)} %copy-done.196), channel_id=1, source_target_pairs={{0,4},{4,0},{8,12},{12,8},{1,5},{5,1},{9,13},{13,9},{2,6},{6,2},{1... | collective-permute-start | bytes 626696 | tf_op jit(solution)/shard_map/ppermute | solution.py:82
  956.8 26.5 %collective-permute-start.185 = (bf16[272,768]{1,0:T(8,128)(2,1)}, bf16[272,768]{1,0:T(8,128)(2,1)}, u32[]{:S(2)}, u32[]{:S(2)}) collective-permute-start(bf16[272,768]{1,0:T(8,128)(2,1)} %pad_maximum_fusion.15), channel_id=1, source_target_pairs={{0,8},{4,12},{8,0},{12,4},{1,9},{5,13},{9,1},{13,5},{2,10},{6,14},... | collective-permute-start | bytes 1253384 | tf_op jit(solution)/shard_map/ppermute | solution.py:91
  983.2 197.3 %collective-permute-start.211 = (bf16[16,768,768]{2,1,0:T(8,128)(2,1)}, bf16[16,768,768]{2,1,0:T(8,128)(2,1)}, u32[]{:S(2)}, u32[]{:S(2)}) collective-permute-start(bf16[16,768,768]{2,1,0:T(8,128)(2,1)} %get-tuple-element.222), channel_id=1, source_target_pairs={{0,16},{16,0},{1,17},{17,1},{2,18},{18,2},{3,19},{19,3},{4,20},{20... | collective-permute-start | bytes 56623112 | tf_op jit(solution)/shard_map/ppermute | solution.py:38
  1033.4 23.3 %collective-permute-start.187 = (bf16[256,768]{1,0:T(8,128)(2,1)}, bf16[256,768]{1,0:T(8,128)(2,1)}, u32[]{:S(2)}, u32[]{:S(2)}) collective-permute-start(bf16[256,768]{1,0:T(8,128)(2,1)} %get-tuple-element.286), channel_id=1, source_target_pairs={{0,2},{1,3},{2,0},{3,1},{4,6},{5,7},{6,4},{7,5},{8,10},{9,11},{10,... | collective-permute-start | bytes 1179656 | tf_op jit(solution)/shard_map/ppermute | solution.py:43
  1073.3 139.3 %collective-permute-start.212 = (bf16[16,768,768]{2,1,0:T(8,128)(2,1)}, bf16[16,768,768]{2,1,0:T(8,128)(2,1)}, u32[]{:S(2)}, u32[]{:S(2)}) collective-permute-start(bf16[16,768,768]{2,1,0:T(8,128)(2,1)} %get-tuple-element.224), channel_id=1, source_target_pairs={{0,16},{16,0},{1,17},{17,1},{2,18},{18,2},{3,19},{19,3},{4,20},{20... | collective-permute-start | bytes 56623112 | tf_op jit(solution)/shard_map/ppermute | solution.py:38
  1073.3 49.8 %collective-permute-start.106 = (f32[256,768]{1,0:T(8,128)}, f32[256,768]{1,0:T(8,128)}, u32[]{:S(2)}, u32[]{:S(2)}) collective-permute-start(f32[256,768]{1,0:T(8,128)} %get-tuple-element.290), channel_id=1, source_target_pairs={{0,16},{16,0},{1,17},{17,1},{2,18},{18,2},{3,19},{19,3},{4,20},{20... | collective-permute-start | bytes 2359304 | tf_op jit(solution)/shard_map/ppermute | solution.py:38
  1155.1 21.8 %collective-permute-start.201 = (bf16[56,3072]{1,0:T(8,128)(2,1)S(1)}, bf16[56,3072]{1,0:T(8,128)(2,1)S(1)}, u32[]{:S(2)}, u32[]{:S(2)}) collective-permute-start(bf16[56,3072]{1,0:T(8,128)(2,1)S(1)} %get-tuple-element.269), channel_id=1, source_target_pairs={{0,2},{1,3},{2,0},{3,1},{4,6},{5,7},{6,4},{7,5},{8,10},{9,11},{10,... | collective-permute-start | bytes 1032200 | tf_op jit(solution)/shard_map/ppermute | solution.py:43
  (394 other events, 5970.6 us)
Sparse Core Ops, SparseCore 0:
  102.8 71.5 all-gather.2
